TPU v7x, 128 devices: a whole 4x4x4 slice. The times are simulated.
128 devices in a mesh: sec: 4 (over z), dev: 32 (over x, y, core).
Axes of the slice: x: 4, y: 4, z: 4, core: 2. Of those that a mesh axis runs over, the one named last changes fastest.
Arguments:
- queries: bfloat16 [256, 128, 576], P(('sec', 'dev')), may hold values from -480 to 480
- latent_cache: bfloat16 [256, 1024, 576], P(('sec', 'dev')), may hold values from -4 to 4
- cache_lengths: int32 [256], P(('sec', 'dev')), may hold values from 2 to 1024, as said below
- expert_input: bfloat16 [1024, 7168], P(('sec', 'dev')), may hold values from -6 to 6
- expert_ids: int32 [1024, 8], P(('sec', 'dev')), may hold values from 0 to 31, all different within a row; in each aligned block of 8 rows (0 to 7, 8 to 15, ...) at most 3 rows name the same one
- route_gates: bfloat16 [1024, 8], P(('sec', 'dev')), may hold values from 0.099609375 to 1
- gate_weight: bfloat16 [7168, 65536], P(None, ('sec', 'dev')), may hold values from -0.0625 to 0.0625
- up_weight: bfloat16 [7168, 65536], P(None, ('sec', 'dev')), may hold values from -0.0625 to 0.0625
- down_weight: bfloat16 [65536, 7168], P(('sec', 'dev')), may hold values from -0.125 to 0.125
Outputs:
- context: bfloat16 [256, 128, 512], P(('sec', 'dev'))
- expert_output: bfloat16 [1024, 7168], P(('sec', 'dev'))
Inputs may be any that keep to these rules, and one draw needn't show every extreme that they name: `cache_lengths`: the first of each device's 2 rows sees all 1024 positions. `expert_ids`: each row names 8 different experts. Among the rows of one device no expert is named by more than 3 rows, and in every draw some expert is named by exactly 3 rows of some device.
All inputs are finite; a program needn't handle non-finite values.
Results may differ from a plain program's by a relative error of at most 0.005.
Values may be sent and summed in bfloat16 or wider, within the bound.
No kernel may reach another device: no remote copies, remote signals or barrier semaphores. Data moves between devices by JAX's collectives and lax.ppermute only.
A program may use at most 128 MiB of HBM per device.

v0:
```python
import jax
import jax.numpy as jnp
from jax import lax
from jax.sharding import PartitionSpec as P

LAT = 512
ROPE = 64
NOPE = 128
EXPERTS = 32
CAP = 3


def attention_rows(queries, latent_cache, cache_lengths):
    scores = jnp.einsum(
        "rhq,rjq->rhj", queries, latent_cache, preferred_element_type=jnp.float32
    ) * (NOPE + ROPE) ** (-0.5)
    positions = jnp.arange(latent_cache.shape[1], dtype=jnp.int32)
    visible = (positions[None, :] < cache_lengths[:, None])[:, None, :]
    highest = jnp.max(jnp.where(visible, scores, -jnp.inf), axis=2, keepdims=True)
    powers = jnp.where(visible, jnp.exp(scores - highest), 0.0)
    attention_weights = (powers / jnp.sum(powers, axis=2, keepdims=True)).astype(jnp.bfloat16)
    latents = latent_cache[:, :, :LAT]
    return jnp.einsum(
        "rhj,rjl->rhl", attention_weights, latents, preferred_element_type=jnp.float32
    ).astype(jnp.bfloat16)


def slot_tables(expert_ids, route_gates):
    chosen = expert_ids[:, :, None] == jnp.arange(EXPERTS, dtype=jnp.int32)[None, None, :]
    member = jnp.sum(chosen.astype(jnp.int32), axis=1)
    earlier = jnp.cumsum(member, axis=0) - member
    placed = (earlier[:, :, None] == jnp.arange(CAP, dtype=jnp.int32)[None, None, :]) & (
        member[:, :, None] > 0
    )
    row_gate = jnp.sum(jnp.where(chosen, route_gates.astype(jnp.float32)[:, :, None], 0.0), axis=1)
    weighted = jnp.where(placed, row_gate[:, :, None], 0.0)
    return (placed, weighted)


def expert_rows(received, gate_weight, up_weight, down_weight):
    flattened = received.reshape(-1, received.shape[-1])
    gate_part = jnp.dot(flattened, gate_weight, preferred_element_type=jnp.float32)
    up_part = jnp.dot(flattened, up_weight, preferred_element_type=jnp.float32)
    active = (jax.nn.silu(gate_part) * up_part).astype(jnp.bfloat16)
    partial_value = jnp.dot(active, down_weight, preferred_element_type=jnp.float32)
    return partial_value.reshape(received.shape[:-1] + (partial_value.shape[-1],))


def gated_rows(returned, weighted, slices):
    row_count = weighted.shape[0]
    model_width = returned.shape[-1]
    summed = (
        returned.reshape(EXPERTS, slices, CAP, model_width)
        .sum(axis=1)
        .reshape(EXPERTS * CAP, model_width)
    )
    merged = jnp.dot(
        weighted.reshape(row_count, EXPERTS * CAP),
        summed,
        precision=lax.Precision.HIGHEST,
        preferred_element_type=jnp.float32,
    )
    return merged.astype(jnp.bfloat16)


def per_device(
    queries,
    latent_cache,
    cache_lengths,
    expert_input,
    expert_ids,
    route_gates,
    gate_weight,
    up_weight,
    down_weight,
):
    context = attention_rows(queries, latent_cache, cache_lengths)
    row_count, model_width = expert_input.shape
    devices = lax.axis_size(("sec", "dev"))
    slices = devices // EXPERTS
    placed, weighted = slot_tables(expert_ids, route_gates)
    assign = jnp.transpose(placed, (1, 2, 0)).reshape(EXPERTS * CAP, row_count).astype(jnp.bfloat16)
    buffer = jnp.dot(assign, expert_input, preferred_element_type=jnp.float32).astype(jnp.bfloat16)
    outgoing = jnp.broadcast_to(
        buffer.reshape(EXPERTS, 1, CAP, model_width), (EXPERTS, slices, CAP, model_width)
    )
    outgoing = outgoing.reshape(devices, CAP, model_width)
    returned = lax.all_to_all(
        expert_rows(
            lax.all_to_all(outgoing, ("sec", "dev"), split_axis=0, concat_axis=0, tiled=True),
            gate_weight,
            up_weight,
            down_weight,
        ),
        ("sec", "dev"),
        split_axis=0,
        concat_axis=0,
        tiled=True,
    )
    expert_output = gated_rows(returned, weighted, slices)
    return (context, expert_output)


def solution(mesh):
    return jax.shard_map(
        per_device,
        mesh=mesh,
        in_specs=(
            P(("sec", "dev"), None, None),
            P(("sec", "dev"), None, None),
            P(("sec", "dev")),
            P(("sec", "dev"), None),
            P(("sec", "dev"), None),
            P(("sec", "dev"), None),
            P(None, ("sec", "dev")),
            P(None, ("sec", "dev")),
            P(("sec", "dev"), None),
        ),
        out_specs=(P(("sec", "dev"), None, None), P(("sec", "dev"), None)),
        check_vma=False,
    )
```

profile of v0, /device:TPU:50, one launch (start us, length us, event | category | flops | bytes accessed | tf_op | source)
XLA Modules:
  0.0 364.2 jit_solution(6227795394146489838)
XLA Ops:
  0.6 0.0 copy-start
  0.6 0.8 convert_reduce_fusion
  1.5 0.1 copy.22
  1.6 0.1 copy.23
  1.8 0.1 eq.49
  1.9 1.5 convolution_convert_fusion
  3.4 0.9 broadcast_in_dim.68
  4.2 5.3 %broadcast_in_dim.69 = bf16[32,4,3,7168]{3,2,1,0:T(4,128)(2,1)} broadcast(bf16[32,3,7168]{2,1,0:T(4,128)(2,1)S(1)} %broadcast_in_dim.68), dimensions={0,2,3} | broadcast | bytes 6881280 | tf_op jit(solution)/shard_map/broadcast_in_dim | solution.py:84
  9.5 92.5 %all_to_all.10 = bf16[128,3,7168]{2,1,0:T(4,128)(2,1)} all-to-all(bf16[128,3,7168]{2,1,0:T(4,128)(2,1)} %bitcast.19), channel_id=1, replica_groups=mesh['sec'=4,'dev'=32] {'sec','dev'}, dimensions={0} | all-to-all | bytes 11010048 | tf_op jit(solution)/shard_map/all_to_all | solution.py:90
  102.0 13.2 %reshape.60 = bf16[384,7168]{1,0:T(8,128)(2,1)} reshape(bf16[128,3,7168]{2,1,0:T(4,128)(2,1)} %all_to_all.10) | data formatting | bytes 11010048 | tf_op jit(solution)/shard_map/reshape | solution.py:41
  115.2 7.1 %fusion.33 = f32[384,512]{1,0:T(8,128)S(1)} fusion(bf16[384,7168]{1,0:T(8,128)(2,1)} %reshape.60, bf16[7168,512]{1,0:T(8,128)(2,1)} %param.15), kind=kOutput, calls=%fused_computation.39 | convolution fusion | flops 2818572288 | bytes 13631488 | tf_op jit(solution)/shard_map/dot_general | solution.py:42
  122.3 0.0 slice-done.2
  122.3 0.0 copy-done.1
  122.3 0.4 slice-done.3
  122.7 3.1 fusion.13
  125.8 0.0 slice-done
  125.8 0.0 slice-done.1
  125.9 5.8 %fusion.34 = f32[384,7168]{1,0:T(8,128)} fusion(bf16[384,512]{1,0:T(8,128)(2,1)S(1)} %fusion.13, bf16[512,7168]{1,0:T(8,128)(2,1)S(1)} %bitcast.21), kind=kOutput, calls=%fused_computation.40 | convolution fusion | flops 2818572288 | bytes 18743296 | tf_op jit(solution)/shard_map/dot_general | solution.py:45
  131.6 16.2 %reshape.61 = f32[128,3,7168]{2,1,0:T(4,128)} reshape(f32[384,7168]{1,0:T(8,128)} %fusion.34) | data formatting | bytes 22020096 | tf_op jit(solution)/shard_map/reshape | solution.py:46
  147.8 10.4 %all-to-all-start.1 = ((f32[128,3,7168]{2,1,0:T(4,128)}), f32[128,3,7168]{2,1,0:T(4,128)}, u32[]{:S(2)}, u32[]{:S(2)}) async-start(f32[128,3,7168]{2,1,0:T(4,128)} %reshape.61), calls=%async_computation.1 | async-start | bytes 29360128 | tf_op jit(solution)/shard_map/all_to_all | solution.py:88
  158.2 0.0 copy-done.4
  158.3 0.0 copy-done.3
  158.3 0.1 select_reduce_fusion.1
  158.4 0.0 copy-done.5
  158.4 0.1 iota_compare_fusion.2
  158.5 0.0 copy-done
  158.5 0.6 convolution_multiply_fusion
  159.1 0.5 fusion.32
  159.7 1.6 fusion.14
  161.2 189.3 %all-to-all-done.1 = f32[128,3,7168]{2,1,0:T(4,128)} async-done(((f32[128,3,7168]{2,1,0:T(4,128)}), f32[128,3,7168]{2,1,0:T(4,128)}, u32[]{:S(2)}, u32[]{:S(2)}) %all-to-all-start.1) | async-done | bytes 11010080 | tf_op jit(solution)/shard_map/all_to_all | solution.py:88
  350.5 9.6 %bitcast_reduce_fusion = f32[32,3,7168]{2,1,0:T(4,128)S(1)} fusion(f32[128,3,7168]{2,1,0:T(4,128)} %all-to-all-done.1), kind=kLoop, calls=%fused_computation.1 | loop fusion | flops 2064384 | bytes 13762560 | tf_op jit(solution)/shard_map/reduce_sum | solution.py:54
  360.1 4.0 %fusion.1 = bf16[8,7168]{1,0:T(8,128)(2,1)} fusion(f32[32,3,7168]{2,1,0:T(4,128)S(1)} %bitcast_reduce_fusion, f32[8,32]{1,0:T(8,128)S(1)} %select_reduce_fusion.1, s32[8,32]{1,0:T(8,128)S(1)} %sub.21, pred[8,32]{1,0:T(8,128)(4,1)S(1)} %broadcast_compare_fusion), kind=kOutput, calls=%fused_computation.4 | convolution fusion | flops 66119936 | bytes 2869504 | tf_op jit(solution)/shard_map/dot_general | solution.py:57
  (22 shorter events, 0.2 us)
Async XLA Ops:
  0.6 157.8 %copy-start = (bf16[2,128,576]{1,2,0:T(8,128)(2,1)S(1)}, bf16[2,128,576]{1,2,0:T(8,128)(2,1)}, u32[]{:S(2)}) copy-start(bf16[2,128,576]{1,2,0:T(8,128)(2,1)} %param.9) | copy-start | bytes 884740
  102.0 20.3 %slice-start.2 = ((s8[7340032]{0:T(1024)(128)(4,1)}), s8[3145728]{0:T(1024)(128)(4,1)S(1)}, s32[]{:S(2)}) async-start(s8[7340032]{0:T(1024)(128)(4,1)} %bitcast.23), calls=%async_computation.4 | async-start | bytes 6291456
  115.2 7.1 %copy-start.1 = (bf16[384,7168]{1,0:T(8,128)(2,1)S(1)}, bf16[384,7168]{1,0:T(8,128)(2,1)}, u32[]{:S(2)}) copy-start(bf16[384,7168]{1,0:T(8,128)(2,1)} %reshape.60) | copy-start | bytes 16515076
  115.2 7.5 %slice-start.3 = ((s8[7340032]{0:T(1024)(128)(4,1)}), s8[4194304]{0:T(1024)(128)(4,1)S(1)}, s32[]{:S(2)}) async-start(s8[7340032]{0:T(1024)(128)(4,1)} %bitcast.23), calls=%async_computation.5 | async-start | bytes 8388608
  115.2 10.7 %slice-start = ((s8[7340032]{0:T(1024)(128)(4,1)}), s8[4194304]{0:T(1024)(128)(4,1)S(1)}, s32[]{:S(2)}) async-start(s8[7340032]{0:T(1024)(128)(4,1)} %bitcast.20), calls=%async_computation.2 | async-start | bytes 8388608
  122.7 3.1 slice-start.1
  147.8 10.4 %copy-start.4 = (bf16[8,8]{1,0:T(8,128)(2,1)S(1)}, bf16[8,8]{1,0:T(8,128)(2,1)}, u32[]{:S(2)}) copy-start(bf16[8,8]{1,0:T(8,128)(2,1)} %param.14) | copy-start | bytes 388
  147.8 10.4 %copy-start.3 = (s32[8,8]{1,0:T(8,128)S(1)}, s32[8,8]{1,0:T(8,128)}, u32[]{:S(2)}) copy-start(s32[8,8]{1,0:T(8,128)} %param.13) | copy-start | bytes 772
  147.8 10.6 %copy-start.5 = (s32[2]{0:T(128)S(1)}, s32[2]{0:T(128)}, u32[]{:S(2)}) copy-start(s32[2]{0:T(128)} %param.11) | copy-start | bytes 28
  147.8 10.7 %copy-start.2 = (bf16[2,1024,576]{1,2,0:T(8,128)(2,1)S(1)}, bf16[2,1024,576]{1,2,0:T(8,128)(2,1)}, u32[]{:S(2)}) copy-start(bf16[2,1024,576]{1,2,0:T(8,128)(2,1)} %param.10) | copy-start | bytes 7077892
  147.8 202.7 %all-to-all-start.1 = ((f32[128,3,7168]{2,1,0:T(4,128)}), f32[128,3,7168]{2,1,0:T(4,128)}, u32[]{:S(2)}, u32[]{:S(2)}) async-start(f32[128,3,7168]{2,1,0:T(4,128)} %reshape.61), calls=%async_computation.1 | async-start | bytes 29360128 | tf_op jit(solution)/shard_map/all_to_all | solution.py:88
where the time goes:
time: 365 us; the launch traced here: 364 us
  waiting for transfers between devices  189 us (52%)
  blocking collectives  92.5 us (25%)
  local copies, waits for them, and re-layouts  36.3 us (10%)
  matrix products  23.6 us (6%)
  other arithmetic  11.2 us (3%)
  starting transfers between devices  10.4 us (3%)
    all_to_all x1, waiting for transfers between devices, per_device(): lax.all_to_all(expert_rows(lax.all_to_all(outgoing, ('sec', 'dev'), split...  189 us
    all_to_all x1, blocking collectives, per_device(): lax.all_to_all(outgoing, ('sec', 'dev'), split_axis=0, concat_axis=0, til...  92.5 us
    reshape x1, local copies, waits for them, and re-layouts, expert_rows(): partial_value.reshape(received.shape[:-1] + (partial_value.shape[-1],))  16.2 us
    reshape x1, local copies, waits for them, and re-layouts, expert_rows(): flattened = received.reshape(-1, received.shape[-1])  13.2 us
    all_to_all x1, starting transfers between devices, per_device(): lax.all_to_all(expert_rows(lax.all_to_all(outgoing, ('sec', 'dev'), split...  10.4 us
    reduce_sum x1, other arithmetic, gated_rows(): summed = returned.reshape(EXPERTS, slices, CAP, model_width).sum(axis=1)....  9.63 us
  transfers between devices with their start and end apart: 1, of which 1 were waited for; matrix products, arithmetic and copies ran while one was open for 1% of the time, Pallas kernels for 0%

commit v1 on v0

v1 whole, which is shorter than its diff:
```python
import functools

import jax
import jax.numpy as jnp
import numpy as np
from jax import lax
from jax.experimental import pallas as pl
from jax.experimental.pallas import tpu as pltpu
from jax.sharding import Mesh, PartitionSpec as P

LAT = 512
ROPE = 64
NOPE = 128
EXPERTS = 32
TOP = 8
CAP = 3
D = 7168
ROWS = 8
GROUP = 8
PIECE = D // GROUP
META = 128
SLOTS = GROUP * CAP
CELLS = 16
HELD = CELLS * SLOTS
HIDDEN = 512
ALL = ("z", "x", "y", "c")
BF16 = jnp.bfloat16
F32 = jnp.float32


def attention_rows(queries, latent_cache, cache_lengths):
    scores = jnp.einsum(
        "rhq,rjq->rhj", queries, latent_cache, preferred_element_type=F32
    ) * (NOPE + ROPE) ** (-0.5)
    positions = jnp.arange(latent_cache.shape[1], dtype=jnp.int32)
    visible = (positions[None, :] < cache_lengths[:, None])[:, None, :]
    highest = jnp.max(jnp.where(visible, scores, -jnp.inf), axis=2, keepdims=True)
    powers = jnp.where(visible, jnp.exp(scores - highest), 0.0)
    attention_weights = (powers / jnp.sum(powers, axis=2, keepdims=True)).astype(BF16)
    latents = latent_cache[:, :, :LAT]
    return jnp.einsum(
        "rhj,rjl->rhl", attention_weights, latents, preferred_element_type=F32
    ).astype(BF16)


def slot_constants():
    q = np.arange(2 * HELD)
    h, cell, source, place = q // HELD, q % HELD // SLOTS, q % SLOTS // CAP, q % CAP
    expert_of = (cell * 2 + h)[:, None] == np.arange(EXPERTS)[None, :]
    row = np.arange(GROUP * ROWS)
    same = source[:, None] == row[None, :] // ROWS
    wanted = np.where(same, place[:, None], -2)
    earlier = (row[:, None] // ROWS == row[None, :] // ROWS) & (row[None, :] < row[:, None])
    return (
        jnp.asarray(expert_of, BF16),
        jnp.asarray(wanted, F32),
        jnp.asarray(wanted.T, F32),
        jnp.asarray(earlier, BF16),
    )


def dot(a, b, contract=((1,), (0,))):
    return lax.dot_general(a, b, (contract, ((), ())), preferred_element_type=F32)


def select_kernel(rows_ref, expert_ref, wanted_ref, wanted_t_ref, earlier_ref, send_ref, mix_ref):
    meta = rows_ref[:, PIECE:].astype(F32)
    lane = lax.broadcasted_iota(jnp.int32, (GROUP * ROWS, EXPERTS), 1).astype(F32)
    member = jnp.zeros((GROUP * ROWS, EXPERTS), F32)
    gate = jnp.zeros((GROUP * ROWS, EXPERTS), F32)
    for k in range(TOP):
        hit = meta[:, k : k + 1] == lane
        member = member + jnp.where(hit, 1.0, 0.0)
        gate = gate + jnp.where(hit, meta[:, TOP + k : TOP + k + 1], 0.0)
    rank = dot(earlier_ref[...], member.astype(BF16))
    place = jnp.where(member > 0.0, rank, -1.0).astype(BF16)
    expert = expert_ref[...]
    chosen = dot(expert, place, ((1,), (1,))) == wanted_ref[...]
    chosen_t = dot(place, expert, ((1,), (1,))) == wanted_t_ref[...]
    weight = dot(gate.astype(BF16), expert, ((1,), (1,)))
    mix_ref[...] = jnp.where(chosen_t, weight, 0.0).astype(BF16)
    pick = jnp.where(chosen, 1.0, 0.0).astype(BF16)
    values = rows_ref[:, :PIECE]
    for h in range(2):
        picked = dot(pick[h * HELD : (h + 1) * HELD], values).astype(BF16)
        send_ref[h, 0] = picked
        send_ref[h, 1] = picked


def select_rows(rows):
    return pl.pallas_call(
        select_kernel,
        out_shape=(
            jax.ShapeDtypeStruct((2, 2, HELD, PIECE), BF16),
            jax.ShapeDtypeStruct((GROUP * ROWS, 2 * HELD), BF16),
        ),
        compiler_params=pltpu.CompilerParams(vmem_limit_bytes=40 << 20),
        name="select_rows",
    )(rows, *slot_constants())


def gate_up_kernel(core_ref, got_ref, gate_ref, up_ref, gate_sum_ref, up_sum_ref):
    step = pl.program_id(0)

    @pl.when(step == 0)
    def _():
        gate_sum_ref[...] = jnp.zeros_like(gate_sum_ref)
        up_sum_ref[...] = jnp.zeros_like(up_sum_ref)

    got = got_ref[0]
    gate_sum_ref[...] += dot(got, gate_ref[...])
    up_sum_ref[...] += dot(got, up_ref[...])


def gate_up_first(core, got, gate_weight, up_weight):
    weight_spec = pl.BlockSpec((PIECE, HIDDEN), lambda y, core: (core[0] * 4 + y, 0))
    sum_spec = pl.BlockSpec((HELD, HIDDEN), lambda y, core: (0, 0))
    return pl.pallas_call(
        gate_up_kernel,
        grid_spec=pltpu.PrefetchScalarGridSpec(
            num_scalar_prefetch=1,
            grid=(4,),
            in_specs=[
                pl.BlockSpec((1, HELD, PIECE), lambda y, core: (y, 0, 0)),
                weight_spec,
                weight_spec,
            ],
            out_specs=(sum_spec, sum_spec),
        ),
        out_shape=(jax.ShapeDtypeStruct((HELD, HIDDEN), F32),) * 2,
        compiler_params=pltpu.CompilerParams(vmem_limit_bytes=40 << 20),
        cost_estimate=pl.CostEstimate(
            flops=4 * HELD * HIDDEN * D // 2, bytes_accessed=2 * HIDDEN * D * 2, transcendentals=0
        ),
        name="gate_up_first",
    )(core, got, gate_weight, up_weight)


def hidden_kernel(
    core_ref, got_ref, gate_ref, up_ref, gate_part_ref, up_part_ref, hidden_ref, gate_sum, up_sum
):
    step = pl.program_id(0)

    @pl.when(step == 0)
    def _():
        gate_sum[...] = gate_part_ref[...]
        up_sum[...] = up_part_ref[...]

    got = got_ref[0]
    gate_sum[...] += dot(got, gate_ref[...])
    up_sum[...] += dot(got, up_ref[...])

    @pl.when(step == 3)
    def _():
        hidden_ref[...] = (jax.nn.silu(gate_sum[...]) * up_sum[...]).astype(BF16)


def hidden_rows(core, got, gate_weight, up_weight, gate_part, up_part):
    weight_spec = pl.BlockSpec((PIECE, HIDDEN), lambda y, core: ((1 - core[0]) * 4 + y, 0))
    sum_spec = pl.BlockSpec((HELD, HIDDEN), lambda y, core: (0, 0))
    return pl.pallas_call(
        hidden_kernel,
        grid_spec=pltpu.PrefetchScalarGridSpec(
            num_scalar_prefetch=1,
            grid=(4,),
            in_specs=[
                pl.BlockSpec((1, HELD, PIECE), lambda y, core: (y, 0, 0)),
                weight_spec,
                weight_spec,
                sum_spec,
                sum_spec,
            ],
            out_specs=sum_spec,
            scratch_shapes=[pltpu.VMEM((HELD, HIDDEN), F32)] * 2,
        ),
        out_shape=jax.ShapeDtypeStruct((HELD, HIDDEN), BF16),
        compiler_params=pltpu.CompilerParams(vmem_limit_bytes=40 << 20),
        cost_estimate=pl.CostEstimate(
            flops=4 * HELD * HIDDEN * D // 2, bytes_accessed=2 * HIDDEN * D * 2, transcendentals=0
        ),
        name="hidden_rows",
    )(core, got, gate_weight, up_weight, gate_part, up_part)


def down_kernel(core_ref, hidden_ref, down_ref, *refs):
    made = dot(hidden_ref[...], down_ref[...])
    if len(refs) == 2:
        made = made + refs[0][0].astype(F32)
    refs[-1][0] = made.astype(BF16)


def down_rows(core, hidden, down_weight, other=None):
    own = other is not None

    def columns(y, core):
        return (0, (core[0] if own else 1 - core[0]) * 4 + y)

    block = pl.BlockSpec((1, HELD, PIECE), lambda y, core: (y, 0, 0))
    return pl.pallas_call(
        down_kernel,
        grid_spec=pltpu.PrefetchScalarGridSpec(
            num_scalar_prefetch=1,
            grid=(4,),
            in_specs=[
                pl.BlockSpec((HELD, HIDDEN), lambda y, core: (0, 0)),
                pl.BlockSpec((HIDDEN, PIECE), columns),
            ]
            + [block] * own,
            out_specs=block,
        ),
        out_shape=jax.ShapeDtypeStruct((4, HELD, PIECE), BF16),
        compiler_params=pltpu.CompilerParams(vmem_limit_bytes=40 << 20),
        cost_estimate=pl.CostEstimate(
            flops=HELD * HIDDEN * D, bytes_accessed=HIDDEN * D, transcendentals=0
        ),
        name="down_own" if own else "down_partner",
    )(core, hidden, down_weight, *((other,) if own else ()))


def combine_kernel(mix_ref, got_ref, out_ref):
    total = jnp.zeros((GROUP * ROWS, PIECE), F32)
    for y in range(4):
        total = total + dot(mix_ref[:, y // 2 * HELD : (y // 2 + 1) * HELD], got_ref[y])
    out_ref[...] = total.astype(BF16)


def combine_rows(mix, got):
    return pl.pallas_call(
        combine_kernel,
        out_shape=jax.ShapeDtypeStruct((GROUP * ROWS, PIECE), BF16),
        compiler_params=pltpu.CompilerParams(vmem_limit_bytes=40 << 20),
        name="combine_rows",
    )(mix, got)


def exchange(values, axes):
    return lax.all_to_all(values, axes, split_axis=0, concat_axis=0, tiled=True)


def swap_cores(values):
    return lax.ppermute(values, "c", [(0, 1), (1, 0)])


def expert_rows(expert_input, expert_ids, route_gates, gate_weight, up_weight, down_weight):
    core = lax.axis_index("c").reshape(1)
    pieces = jnp.transpose(expert_input.reshape(ROWS, 2, 4, PIECE), (2, 1, 0, 3))
    meta = jnp.concatenate([expert_ids.astype(BF16), route_gates], axis=1)
    meta = jnp.pad(meta, ((0, 0), (0, META - 2 * TOP)))
    meta = jnp.broadcast_to(meta[None], (GROUP, ROWS, META))
    outgoing = jnp.concatenate([pieces.reshape(GROUP, ROWS, PIECE), meta], axis=2)
    shared = exchange(outgoing, ("y", "c")).reshape(GROUP * ROWS, PIECE + META)

    send, mix = select_rows(shared)
    send = send.reshape(4 * CELLS, SLOTS, PIECE)
    got = exchange(send, ("y", "z", "x")).reshape(4, HELD, PIECE)
    got_other = swap_cores(got)
    gate_part, up_part = gate_up_first(core, got, gate_weight, up_weight)
    hidden = hidden_rows(core, got_other, gate_weight, up_weight, gate_part, up_part)
    other = swap_cores(down_rows(core, hidden, down_weight))
    made = down_rows(core, hidden, down_weight, other)
    made = made.reshape(4 * CELLS, SLOTS, PIECE)
    returned = exchange(made, ("y", "z", "x")).reshape(4, HELD, PIECE)

    merged = combine_rows(mix, returned).reshape(GROUP, ROWS, PIECE)
    pieces = exchange(merged, ("y", "c")).reshape(4, 2, ROWS, PIECE)
    return jnp.transpose(pieces, (2, 1, 0, 3)).reshape(ROWS, D)


def per_device(
    queries,
    latent_cache,
    cache_lengths,
    expert_input,
    expert_ids,
    route_gates,
    gate_weight,
    up_weight,
    down_weight,
):
    context = attention_rows(queries, latent_cache, cache_lengths)
    expert_output = expert_rows(
        expert_input, expert_ids, route_gates, gate_weight, up_weight, down_weight
    )
    return (context, expert_output)


def solution(mesh):
    chips = Mesh(mesh.devices.reshape(4, 4, 4, 2), ALL)
    return jax.shard_map(
        per_device,
        mesh=chips,
        in_specs=(
            P(ALL, None, None),
            P(ALL, None, None),
            P(ALL),
            P(ALL, None),
            P(ALL, None),
            P(ALL, None),
            P(None, ALL),
            P(None, ALL),
            P(ALL, None),
        ),
        out_specs=(P(ALL, None, None), P(ALL, None)),
        check_vma=False,
    )
```

time: 365 us -> 151 us (0.41)
  the two profiles are of different devices: /device:TPU:50 before, /device:TPU:0 now
where the time goes in v1:
time: 151 us; the launch traced here: 149 us
  blocking collectives  56.8 us (38%)
  waiting for transfers between devices  42.8 us (28%)
  Pallas kernels  20.4 us (14%)
  local copies, waits for them, and re-layouts  11.4 us (8%)
  starting transfers between devices  8.8 us (6%)
  matrix products  5.76 us (4%)
  other arithmetic  2.78 us (2%)
    all_to_all x2, blocking collectives, exchange(): return lax.all_to_all(values, axes, split_axis=0, concat_axis=0, tiled=True)  56.8 us
    all_to_all x2, waiting for transfers between devices, exchange(): return lax.all_to_all(values, axes, split_axis=0, concat_axis=0, tiled=True)  38.1 us
    unnamed x20, local copies, waits for them, and re-layouts  9.75 us
    all_to_all x2, starting transfers between devices, exchange(): return lax.all_to_all(values, axes, split_axis=0, concat_axis=0, tiled=True)  8.22 us
    pallas_call x2, Pallas kernels, down_rows(): pl.pallas_call(down_kernel, grid_spec=pltpu.PrefetchScalarGridSpec(num_sc...  6.46 us
    pallas_call x1, Pallas kernels, hidden_rows(): pl.pallas_call(hidden_kernel, grid_spec=pltpu.PrefetchScalarGridSpec(num_...  6.24 us
    pallas_call x1, Pallas kernels, gate_up_first(): pl.pallas_call(gate_up_kernel, grid_spec=pltpu.PrefetchScalarGridSpec(num...  5.63 us
    ppermute x2, waiting for transfers between devices, swap_cores(): return lax.ppermute(values, 'c', [(0, 1), (1, 0)])  4.73 us
  transfers between devices with their start and end apart: 4, of which 3 were waited for; matrix products, arithmetic and copies ran while one was open for 5% of the time, Pallas kernels for 4%

profile of v1, /device:TPU:0, one launch (start us, length us, event | category | flops | bytes accessed | tf_op | source)
XLA Modules:
  0.0 149.5 jit_solution(7376412888969013058)
XLA Ops:
  0.6 0.0 copy-start
  0.6 1.0 copy.16
  1.6 0.7 convert_element_type.13
  2.3 0.8 fusion.19
  3.1 10.5 %all_to_all.20 = bf16[8,8,1024]{2,1,0:T(8,128)(2,1)S(1)} all-to-all(bf16[8,8,1024]{2,1,0:T(8,128)(2,1)S(1)} %pad_maximum_fusion), channel_id=1, replica_groups=mesh['z'=4,'x'=4,'y'=4,'c'=2] {'y','c'}, dimensions={0} | all-to-all | bytes 262144 | tf_op jit(solution)/shard_map/all_to_all | solution.py:237
  13.6 1.0 copy-done.3
  14.6 0.9 copy-done.4
  15.5 0.9 copy-done.5
  16.4 0.7 copy-done.6
  17.1 0.9 select_rows.1
  18.0 46.3 %all_to_all.21 = bf16[64,24,896]{2,1,0:T(8,128)(2,1)S(1)} all-to-all(bf16[64,24,896]{2,1,0:T(8,128)(2,1)S(1)} %bitcast.22), channel_id=1, replica_groups=mesh['z'=4,'x'=4,'y'=4,'c'=2] {'y','z','x'}, dimensions={0} | all-to-all | bytes 5505024 | tf_op jit(solution)/shard_map/all_to_all | solution.py:237
  64.3 0.0 collective-permute-start
  64.3 3.1 %copy-done.1 = bf16[7168,512]{1,0:T(8,128)(2,1)S(1)} copy-done((bf16[7168,512]{1,0:T(8,128)(2,1)S(1)}, bf16[7168,512]{1,0:T(8,128)(2,1)}, u32[]{:S(2)}) %copy-start.1) | copy-done | bytes 7340056
  67.4 5.6 %gate_up_first.1 = (f32[384,512]{1,0:T(8,128)S(1)}, f32[384,512]{1,0:T(8,128)S(1)}) custom-call(s32[1]{0:T(128)} %bitcast.4.core_ref, bf16[4,384,896]{2,1,0:T(8,128)(2,1)S(1)} %bitcast.20, bf16[7168,512]{1,0:T(8,128)(2,1)S(1)} %copy-done.1, bf16[7168,512]{1,0:T(8,128)(2,1)} %up_ref.3), custom_call_target="tpu_custom_call" | custom-call | flops 2818572288 | bytes 14680064 | tf_op jit(solution)/shard_map/gate_up_first/pallas_call | solution.py:118
  73.1 0.0 collective-permute-done.got_ref
  73.1 0.0 copy-start.2
  73.1 3.1 %copy-done.2 = bf16[7168,512]{1,0:T(8,128)(2,1)S(1)} copy-done((bf16[7168,512]{1,0:T(8,128)(2,1)S(1)}, bf16[7168,512]{1,0:T(8,128)(2,1)}, u32[]{:S(2)}) %copy-start.2) | copy-done | bytes 7340056
  76.2 6.2 %hidden_rows.1.hidden_ref = bf16[384,512]{1,0:T(8,128)(2,1)S(1)} custom-call(s32[1]{0:T(128)} %bitcast.4.core_ref, bf16[4,384,896]{2,1,0:T(8,128)(2,1)} %collective-permute-done.got_ref, bf16[7168,512]{1,0:T(8,128)(2,1)S(1)} %copy-done.2, bf16[7168,512]{1,0:T(8,128)(2,1)} %up_ref.3, f32[384,512]{1,0:T(8,128)S(1)} %get-tuple-element.8.gate_part_ref, ...), custom_call_target="tpu_custom_call" | custom-call | flops 2818572288 | bytes 14680064 | tf_op jit(solution)/shard_map/hidden_rows/pallas_call | solution.py:161
  82.4 2.7 %down_partner.1 = bf16[4,384,896]{2,1,0:T(8,128)(2,1)S(1)} custom-call(s32[1]{0:T(128)} %bitcast.4.core_ref, bf16[384,512]{1,0:T(8,128)(2,1)S(1)} %hidden_rows.1.hidden_ref, bf16[512,7168]{1,0:T(8,128)(2,1)S(1)} %bitcast.18), custom_call_target="tpu_custom_call" | custom-call | flops 1409286144 | bytes 3670016 | tf_op jit(solution)/shard_map/down_partner/pallas_call | solution.py:199
  85.2 0.6 collective-permute-start.1
  85.8 4.7 %collective-permute-done.1.refs_0_ = bf16[4,384,896]{2,1,0:T(8,128)(2,1)S(1)} collective-permute-done((bf16[4,384,896]{2,1,0:T(8,128)(2,1)S(1)}, bf16[4,384,896]{2,1,0:T(8,128)(2,1)S(1)}, u32[]{:S(2)}, u32[]{:S(2)}) %collective-permute-start.1) | collective-permute-done | bytes 2752544 | tf_op jit(solution)/shard_map/ppermute | solution.py:241
  90.5 3.7 %down_own.1 = bf16[4,384,896]{2,1,0:T(8,128)(2,1)} custom-call(s32[1]{0:T(128)} %bitcast.4.core_ref, bf16[384,512]{1,0:T(8,128)(2,1)S(1)} %hidden_rows.1.hidden_ref, bf16[512,7168]{1,0:T(8,128)(2,1)S(1)} %bitcast.18, bf16[4,384,896]{2,1,0:T(8,128)(2,1)S(1)} %collective-permute-done.1.refs_0_), custom_call_target="tpu_custom_call" | custom-call | flops 1409286144 | bytes 3670016 | tf_op jit(solution)/shard_map/down_own/pallas_call | solution.py:199
  94.2 4.9 %all-to-all-start.2 = ((bf16[64,24,896]{2,1,0:T(8,128)(2,1)}), bf16[64,24,896]{2,1,0:T(8,128)(2,1)S(1)}, u32[]{:S(2)}, u32[]{:S(2)}) async-start(bf16[64,24,896]{2,1,0:T(8,128)(2,1)} %bitcast.7), calls=%async_computation.2 | async-start | bytes 5505024 | tf_op jit(solution)/shard_map/all_to_all | solution.py:237
  99.1 0.1 iota_compare_fusion
  99.1 2.3 %convolution_multiply_fusion = f32[2,128,1024]{2,1,0:T(8,128)S(1)} fusion(bf16[2,128,576]{1,2,0:T(8,128)(2,1)S(1)} %copy-done, bf16[2,1024,576]{1,2,0:T(8,128)(2,1)} %param.14), kind=kOutput, calls=%fused_computation.8 | convolution fusion | flops 302252032 | bytes 3702784 | tf_op jit(solution)/shard_map/rhq,rjq->rhj/dot_general | solution.py:32
  101.5 1.2 fusion.21
  102.7 35.7 %all-to-all-done.2 = bf16[64,24,896]{2,1,0:T(8,128)(2,1)S(1)} async-done(((bf16[64,24,896]{2,1,0:T(8,128)(2,1)}), bf16[64,24,896]{2,1,0:T(8,128)(2,1)S(1)}, u32[]{:S(2)}, u32[]{:S(2)}) %all-to-all-start.2) | async-done | bytes 2752544 | tf_op jit(solution)/shard_map/all_to_all | solution.py:237
  138.4 1.2 combine_rows.1
  139.6 3.4 %all-to-all-start.3 = ((bf16[8,8,896]{2,1,0:T(8,128)(2,1)}), bf16[8,8,896]{2,1,0:T(8,128)(2,1)S(1)}, u32[]{:S(2)}, u32[]{:S(2)}) async-start(bf16[8,8,896]{2,1,0:T(8,128)(2,1)} %bitcast.9), calls=%async_computation.3 | async-start | bytes 229376 | tf_op jit(solution)/shard_map/all_to_all | solution.py:237
  142.9 3.5 %fusion.11 = bf16[2,128,512]{2,1,0:T(8,128)(2,1)} fusion(bf16[2,1024,576]{1,2,0:T(8,128)(2,1)} %param.14, f32[2,128,1024]{2,1,0:T(8,128)} %get-tuple-element.11, f32[2,128]{1,0:T(2,128)S(1)} %get-tuple-element.10), kind=kOutput, calls=%fused_computation.9 | convolution fusion | flops 269090816 | bytes 3408896 | tf_op jit(solution)/shard_map/rhj,rjl->rhl/dot_general | solution.py:41
  146.4 2.4 %all-to-all-done.3 = bf16[8,8,896]{2,1,0:T(8,128)(2,1)S(1)} async-done(((bf16[8,8,896]{2,1,0:T(8,128)(2,1)}), bf16[8,8,896]{2,1,0:T(8,128)(2,1)S(1)}, u32[]{:S(2)}, u32[]{:S(2)}) %all-to-all-start.3) | async-done | bytes 114720 | tf_op jit(solution)/shard_map/all_to_all | solution.py:237
  148.8 0.7 copy.17
  (15 shorter events, 0.0 us)
Async XLA Ops:
  0.6 98.5 %copy-start = (bf16[2,128,576]{1,2,0:T(8,128)(2,1)S(1)}, bf16[2,128,576]{1,2,0:T(8,128)(2,1)}, u32[]{:S(2)}) copy-start(bf16[2,128,576]{1,2,0:T(8,128)(2,1)} %param.13) | copy-start | bytes 884740
  13.6 1.0 copy-start.3
  14.6 0.9 copy-start.4
  15.5 0.9 copy-start.5
  16.4 0.7 copy-start.6
  64.3 8.7 %collective-permute-start = (bf16[4,384,896]{2,1,0:T(8,128)(2,1)S(1)}, bf16[4,384,896]{2,1,0:T(8,128)(2,1)}, u32[]{:S(2)}, u32[]{:S(2)}) collective-permute-start(bf16[4,384,896]{2,1,0:T(8,128)(2,1)S(1)} %bitcast.19), channel_id=1, source_target_pairs={{0,1},{1,0},{2,3},{3,2},{4,5},{5,4},{6,7},{7,6},{8,9},{9,8},{10,11... | collective-permute-start | bytes 8257544 | tf_op jit(solution)/shard_map/ppermute | solution.py:241
  64.3 3.1 %copy-start.1 = (bf16[7168,512]{1,0:T(8,128)(2,1)S(1)}, bf16[7168,512]{1,0:T(8,128)(2,1)}, u32[]{:S(2)}) copy-start(bf16[7168,512]{1,0:T(8,128)(2,1)} %gate_ref.3) | copy-start | bytes 22020100
  67.4 15.0 %slice-start = ((s8[7340032]{0:T(1024)(128)(4,1)}), s8[4194304]{0:T(1024)(128)(4,1)S(1)}, s32[]{:S(2)}) async-start(s8[7340032]{0:T(1024)(128)(4,1)} %bitcast.17), calls=%async_computation.4 | async-start | bytes 8388608
  73.1 3.1 %copy-start.2 = (bf16[7168,512]{1,0:T(8,128)(2,1)S(1)}, bf16[7168,512]{1,0:T(8,128)(2,1)}, u32[]{:S(2)}) copy-start(bf16[7168,512]{1,0:T(8,128)(2,1)} %gate_ref.3) | copy-start | bytes 22020100
  76.1 6.3 %slice-start.1 = ((s8[7340032]{0:T(1024)(128)(4,1)}), s8[3145728]{0:T(1024)(128)(4,1)S(1)}, s32[]{:S(2)}) async-start(s8[7340032]{0:T(1024)(128)(4,1)} %bitcast.17), calls=%async_computation.5 | async-start | bytes 6291456
  85.2 5.3 %collective-permute-start.1 = (bf16[4,384,896]{2,1,0:T(8,128)(2,1)S(1)}, bf16[4,384,896]{2,1,0:T(8,128)(2,1)S(1)}, u32[]{:S(2)}, u32[]{:S(2)}) collective-permute-start(bf16[4,384,896]{2,1,0:T(8,128)(2,1)S(1)} %down_partner.1), channel_id=1, source_target_pairs={{0,1},{1,0},{2,3},{3,2},{4,5},{5,4},{6,7},{7,6},{8,9},{9,8},{10,11... | collective-permute-start | bytes 8257544 | tf_op jit(solution)/shard_map/ppermute | solution.py:241
  94.2 4.9 %copy-start.7 = (s32[2]{0:T(128)S(1)}, s32[2]{0:T(128)}, u32[]{:S(2)}) copy-start(s32[2]{0:T(128)} %param.15) | copy-start | bytes 28
  94.2 44.2 %all-to-all-start.2 = ((bf16[64,24,896]{2,1,0:T(8,128)(2,1)}), bf16[64,24,896]{2,1,0:T(8,128)(2,1)S(1)}, u32[]{:S(2)}, u32[]{:S(2)}) async-start(bf16[64,24,896]{2,1,0:T(8,128)(2,1)} %bitcast.7), calls=%async_computation.2 | async-start | bytes 5505024 | tf_op jit(solution)/shard_map/all_to_all | solution.py:237
  139.6 9.3 %all-to-all-start.3 = ((bf16[8,8,896]{2,1,0:T(8,128)(2,1)}), bf16[8,8,896]{2,1,0:T(8,128)(2,1)S(1)}, u32[]{:S(2)}, u32[]{:S(2)}) async-start(bf16[8,8,896]{2,1,0:T(8,128)(2,1)} %bitcast.9), calls=%async_computation.3 | async-start | bytes 229376 | tf_op jit(solution)/shard_map/all_to_all | solution.py:237

commit v2 on v0

v2 whole, which is shorter than its diff:
```python
import jax
import jax.numpy as jnp
from jax import lax
from jax.experimental import pallas as pl
from jax.experimental.pallas import tpu as pltpu
from jax.sharding import Mesh, PartitionSpec as P

LAT = 512
ROPE = 64
NOPE = 128
EXPERTS = 32
TOP = 8
CAP = 3
D = 7168
HIDDEN = 512
ROWS = 8
FOLD = 8
WIDTH = D // FOLD
CELLS = 16
MESSAGE = CAP * FOLD
SENDERS = 64
SLOTS = SENDERS * CAP
CHUNK = 32
TILE = CHUNK * FOLD
ALL = ("z", "x", "y", "c")
BF16 = jnp.bfloat16
F32 = jnp.float32


def attention_rows(queries, latent_cache, cache_lengths):
    scores = jnp.einsum(
        "rhq,rjq->rhj", queries, latent_cache, preferred_element_type=F32
    ) * (NOPE + ROPE) ** (-0.5)
    positions = jnp.arange(latent_cache.shape[1], dtype=jnp.int32)
    visible = (positions[None, :] < cache_lengths[:, None])[:, None, :]
    highest = jnp.max(jnp.where(visible, scores, -jnp.inf), axis=2, keepdims=True)
    powers = jnp.where(visible, jnp.exp(scores - highest), 0.0)
    attention_weights = (powers / jnp.sum(powers, axis=2, keepdims=True)).astype(BF16)
    latents = latent_cache[:, :, :LAT]
    return jnp.einsum(
        "rhj,rjl->rhl", attention_weights, latents, preferred_element_type=F32
    ).astype(BF16)


def dot(a, b, contract=((1,), (0,))):
    return lax.dot_general(a, b, (contract, ((), ())), preferred_element_type=F32)


def array(*shape, dtype=BF16):
    return jax.ShapeDtypeStruct(shape, dtype)


def in_vmem(count):
    return [pl.BlockSpec(memory_space=pltpu.VMEM)] * count


def in_hbm(count):
    return [pl.BlockSpec(memory_space=pltpu.HBM)] * count


def call(kernel, name, out_shape, *operands, limit=12, scalars=0, hbm=0, **settings):
    many = isinstance(out_shape, tuple)
    return pl.pallas_call(
        kernel,
        in_specs=[pl.BlockSpec(memory_space=pltpu.SMEM)] * scalars
        + in_vmem(len(operands) - scalars - hbm)
        + in_hbm(hbm),
        out_specs=tuple(in_vmem(len(out_shape))) if many else in_vmem(1)[0],
        out_shape=out_shape,
        compiler_params=pltpu.CompilerParams(vmem_limit_bytes=limit << 20),
        name=name,
        **settings,
    )(*operands)


def index_of(shape, axis):
    return lax.broadcasted_iota(jnp.int32, shape, axis).astype(F32)


def quotient(values, divisor):
    return jnp.floor((values + 0.5) * (1.0 / divisor))


def remainder(values, divisor):
    return values - quotient(values, divisor) * divisor


def slot_matches(shape, axis):
    q, p = index_of(shape, axis), index_of(shape, 1 - axis)
    place = quotient(remainder(q, MESSAGE), FOLD)
    same_part = remainder(q, FOLD) == quotient(p, ROWS)
    lanes = (2 * CELLS * MESSAGE, EXPERTS)
    q = index_of(lanes, 0)
    h = quotient(q, CELLS * MESSAGE)
    expert = quotient(q - h * (CELLS * MESSAGE), MESSAGE) * 2 + h
    lanes = jnp.where(expert == index_of(lanes, 1), 1.0, 0.0).astype(BF16)
    return lanes, place, same_part


def select_kernel(input_ref, ids_ref, gates_ref, send_ref, mix_ref):
    ids, gates = ids_ref[...].astype(F32), gates_ref[...].astype(F32)
    lane = index_of((ROWS, EXPERTS), 1)
    member = jnp.zeros(lane.shape, F32)
    gate = jnp.zeros(lane.shape, F32)
    for k in range(TOP):
        hit = ids[:, k : k + 1] == lane
        member = member + jnp.where(hit, 1.0, 0.0)
        gate = gate + jnp.where(hit, gates[:, k : k + 1], 0.0)
    earlier = index_of((ROWS, ROWS), 1) < index_of((ROWS, ROWS), 0)
    rank = dot(jnp.where(earlier, 1.0, 0.0), member)
    place = jnp.where(member > 0.0, rank, -1.0)
    place = jnp.concatenate([place] * FOLD, axis=0).astype(BF16)
    gate = jnp.concatenate([gate] * FOLD, axis=0).astype(BF16)
    folded = jnp.concatenate(
        [input_ref[:, k * WIDTH : (k + 1) * WIDTH] for k in range(FOLD)], axis=0
    )
    half = CELLS * MESSAGE

    lanes, wanted, same_part = slot_matches((2 * half, FOLD * ROWS), 0)
    chosen = (dot(lanes, place, ((1,), (1,))) == wanted) & same_part
    pick = jnp.where(chosen, 1.0, 0.0).astype(BF16)
    for h in range(2):
        picked = dot(pick[h * half : (h + 1) * half], folded).astype(BF16)
        send_ref[h, 0] = picked
        send_ref[h, 1] = picked

    _, wanted, same_part = slot_matches((FOLD * ROWS, 2 * half), 1)
    chosen = (dot(place, lanes, ((1,), (1,))) == wanted) & same_part
    weight = dot(gate, lanes, ((1,), (1,)))
    mix_ref[...] = jnp.where(chosen, weight, 0.0).astype(BF16)


def unfold_kernel(got_ref, rows_ref):
    row, column = index_of((TILE, TILE), 0), index_of((TILE, TILE), 1)
    order = remainder(row, CHUNK) * FOLD + quotient(row, CHUNK) == column
    order = jnp.where(order, 1.0, 0.0).astype(BF16)
    for b in range(SLOTS // CHUNK):
        moved = dot(order, got_ref[b * TILE : (b + 1) * TILE]).astype(BF16)
        for k in range(FOLD):
            rows_ref[b * CHUNK : (b + 1) * CHUNK, k * WIDTH : (k + 1) * WIDTH] = moved[
                k * CHUNK : (k + 1) * CHUNK
            ]


def hidden_kernel(rows_ref, gate_ref, up_ref, hidden_ref):
    gate = dot(rows_ref[...], gate_ref[...])
    up = dot(rows_ref[...], up_ref[...])
    hidden_ref[...] = (jax.nn.silu(gate) * up).astype(BF16)


def down_kernel(own_ref, other_ref, own_down, other_down, made_ref, parts):
    for k in range(FOLD):
        columns = slice(k * WIDTH, (k + 1) * WIDTH)
        made = dot(own_ref[...], own_down[:, columns]) + dot(other_ref[...], other_down[:, columns])
        parts[k] = made.astype(BF16)
    row, column = index_of((TILE, TILE), 0), index_of((TILE, TILE), 1)
    order = remainder(row, FOLD) * CHUNK + quotient(row, FOLD) == column
    order = jnp.where(order, 1.0, 0.0).astype(BF16)
    for b in range(SLOTS // CHUNK):
        rows = [parts[k, b * CHUNK : (b + 1) * CHUNK] for k in range(FOLD)]
        moved = dot(order, jnp.concatenate(rows, axis=0))
        made_ref[b * TILE : (b + 1) * TILE] = moved.astype(BF16)


def combine_kernel(mix_ref, got_ref, out_ref):
    half = CELLS * MESSAGE
    total = jnp.zeros((FOLD * ROWS, WIDTH), F32)
    for y in range(4):
        total = total + dot(mix_ref[:, y // 2 * half : (y // 2 + 1) * half], got_ref[y])
    total = total.astype(BF16)
    for k in range(FOLD):
        out_ref[:, k * WIDTH : (k + 1) * WIDTH] = total[k * ROWS : (k + 1) * ROWS]


def exchange(values):
    values = values.reshape(SENDERS, MESSAGE, WIDTH)
    return lax.all_to_all(values, ("y", "z", "x"), split_axis=0, concat_axis=0, tiled=True)


def swap_cores(values):
    return lax.ppermute(values, "c", [(0, 1), (1, 0)])


def cost(flops, size):
    return pl.CostEstimate(flops=flops, bytes_accessed=size, transcendentals=0)


def expert_rows(
    attention, expert_input, expert_ids, route_gates, gate_weight, up_weight, down_weight
):
    send, mix = call(
        select_kernel, "select",
        (array(2, 2, CELLS * MESSAGE, WIDTH), array(FOLD * ROWS, 2 * CELLS * MESSAGE)),
        expert_input, expert_ids, route_gates,
    )
    got = exchange(send).reshape(SLOTS * FOLD, WIDTH)
    down_other = swap_cores(down_weight)
    rows = call(
        unfold_kernel, "unfold", array(SLOTS, D), got, cost_estimate=cost(8 * 10**9, 4 * SLOTS * D)
    )
    rows_other = swap_cores(rows)
    queries, latent_cache, cache_lengths = attention
    queries, rows = lax.optimization_barrier((queries, rows))
    context = attention_rows(queries, latent_cache, cache_lengths)
    context, rows = lax.optimization_barrier((context, rows))

    flops, size = 4 * SLOTS * D * HIDDEN, 4 * D * HIDDEN
    own, other = (
        call(
            hidden_kernel, "hidden", array(SLOTS, HIDDEN), held, gate_weight, up_weight,
            cost_estimate=cost(flops, size),
        )
        for held in (rows, rows_other)
    )
    made = call(
        down_kernel, "down", array(SLOTS * FOLD, WIDTH),
        own, swap_cores(other), down_weight, down_other, cost_estimate=cost(flops, size),
        scratch_shapes=[pltpu.VMEM((FOLD, SLOTS, WIDTH), BF16)],
    )
    returned = exchange(made).reshape(4, CELLS * MESSAGE, WIDTH)
    return context, call(combine_kernel, "combine", array(ROWS, D), mix, returned)


def per_device(
    queries,
    latent_cache,
    cache_lengths,
    expert_input,
    expert_ids,
    route_gates,
    gate_weight,
    up_weight,
    down_weight,
):
    attention = (queries, latent_cache, cache_lengths)
    return expert_rows(
        attention, expert_input, expert_ids, route_gates, gate_weight, up_weight, down_weight
    )


def solution(mesh):
    chips = Mesh(mesh.devices.reshape(4, 4, 4, 2), ALL)
    return jax.shard_map(
        per_device,
        mesh=chips,
        in_specs=(
            P(ALL, None, None),
            P(ALL, None, None),
            P(ALL),
            P(ALL, None),
            P(ALL, None),
            P(ALL, None),
            P(None, ALL),
            P(None, ALL),
            P(ALL, None),
        ),
        out_specs=(P(ALL, None, None), P(ALL, None)),
        check_vma=False,
    )
```

time: 365 us -> 115 us (0.32)
  the two profiles are of different devices: /device:TPU:50 before, /device:TPU:0 now
where the time goes in v2:
time: 115 us; the launch traced here: 114 us
  blocking collectives  92 us (80%)
  Pallas kernels  13.5 us (12%)
  local copies, waits for them, and re-layouts  2.81 us (2%)
  matrix products  2.18 us (2%)
  waiting for transfers between devices  1.77 us (2%)
    all_to_all x2, blocking collectives, exchange(): lax.all_to_all(values, ('y', 'z', 'x'), split_axis=0, concat_axis=0, tile...  92 us
    pallas_call x6, Pallas kernels, call(): pl.pallas_call(kernel, in_specs=[pl.BlockSpec(memory_space=pltpu.SMEM)] *...  13.5 us
    unnamed x24, local copies, waits for them, and re-layouts  2.81 us
  transfers between devices with their start and end apart: 3, of which 1 were waited for; matrix products, arithmetic and copies ran while one was open for 2% of the time, Pallas kernels for 7%

profile of v2, /device:TPU:0, one launch (start us, length us, event | category | flops | bytes accessed | tf_op | source)
XLA Modules:
  0.0 114.3 jit_solution(8471382802217028941)
XLA Ops:
  0.6 0.0 copy-start
  0.6 0.1 collective-permute-start.2
  0.7 0.0 copy-start.1
  0.8 0.9 copy-done.1
  1.6 0.7 copy-done.2
  2.3 0.7 copy-done.3
  3.0 1.0 select.1
  4.0 0.0 slice-start
  4.1 0.0 slice-start.2
  4.1 49.5 %all_to_all.10 = bf16[64,24,896]{2,1,0:T(8,128)(2,1)S(1)} all-to-all(bf16[64,24,896]{2,1,0:T(8,128)(2,1)S(1)} %bitcast.14), channel_id=1, replica_groups=mesh['z'=4,'x'=4,'y'=4,'c'=2] {'y','z','x'}, dimensions={0} | all-to-all | bytes 5505024 | tf_op jit(solution)/shard_map/all_to_all | solution.py:177
  53.6 1.0 unfold.1.rows_ref
  54.6 0.1 collective-permute-start
  54.7 0.0 copy-done.5
  54.7 0.1 iota_compare_fusion
  54.8 0.0 copy-done
  54.8 0.5 copy-done.4
  55.3 0.6 convolution_multiply_fusion
  55.9 0.5 fusion.18
  56.5 1.5 %fusion.11 = bf16[2,128,512]{2,1,0:T(8,128)(2,1)} fusion(bf16[2,1024,576]{1,2,0:T(8,128)(2,1)S(1)} %copy-done.4, f32[2,128,1024]{2,1,0:T(8,128)S(1)} %get-tuple-element.15, f32[2,128]{1,0:T(2,128)S(1)} %get-tuple-element.14), kind=kOutput, calls=%fused_computation.9 | convolution fusion | flops 269090816 | bytes 3408896 | tf_op jit(solution)/shard_map/rhj,rjl->rhl/dot_general | solution.py:40
  58.0 1.8 %collective-permute-done.rows_ref = bf16[192,7168]{1,0:T(8,128)(2,1)S(1)} collective-permute-done((bf16[192,7168]{1,0:T(8,128)(2,1)S(1)}, bf16[192,7168]{1,0:T(8,128)(2,1)S(1)}, u32[]{:S(2)}, u32[]{:S(2)}) %collective-permute-start) | collective-permute-done | bytes 2752544 | tf_op jit(solution)/shard_map/ppermute | solution.py:181
  59.8 0.0 slice-done
  59.8 0.0 slice-done.1
  59.8 0.0 slice-start.4
  59.8 3.0 %hidden.3 = bf16[192,512]{1,0:T(8,128)(2,1)S(1)} custom-call(bf16[192,7168]{1,0:T(8,128)(2,1)S(1)} %collective-permute-done.rows_ref, bf16[7168,512]{1,0:T(8,128)(2,1)S(1)} %bitcast.7, bf16[7168,512]{1,0:T(8,128)(2,1)S(1)} %bitcast.9), custom_call_target="tpu_custom_call" | custom-call | flops 2818572288 | bytes 14680064 | tf_op jit(solution)/shard_map/hidden/pallas_call | solution.py:63
  62.8 0.0 slice-start.5
  62.9 0.4 collective-permute-start.1
  63.2 3.0 %hidden.2.own_ref = bf16[192,512]{1,0:T(8,128)(2,1)S(1)} custom-call(bf16[192,7168]{1,0:T(8,128)(2,1)S(1)} %unfold.1.rows_ref, bf16[7168,512]{1,0:T(8,128)(2,1)S(1)} %bitcast.7, bf16[7168,512]{1,0:T(8,128)(2,1)S(1)} %bitcast.9), custom_call_target="tpu_custom_call" | custom-call | flops 2818572288 | bytes 14680064 | tf_op jit(solution)/shard_map/hidden/pallas_call | solution.py:63
  66.3 0.0 collective-permute-done.1.other_ref
  66.3 0.0 collective-permute-done.2.other_down
  66.3 4.3 %down.1 = bf16[1536,896]{1,0:T(8,128)(2,1)S(1)} custom-call(bf16[192,512]{1,0:T(8,128)(2,1)S(1)} %hidden.2.own_ref, bf16[192,512]{1,0:T(8,128)(2,1)S(1)} %collective-permute-done.1.other_ref, bf16[512,7168]{1,0:T(8,128)(2,1)S(1)} %bitcast.13, bf16[512,7168]{1,0:T(8,128)(2,1)S(1)} %collective-permute-done.2.other_down), custom_call_target="tpu_custom_call" | custom-call | flops 2818572288 | bytes 14680064 | tf_op jit(solution)/shard_map/down/pallas_call | solution.py:63
  70.6 42.5 %all_to_all.11 = bf16[64,24,896]{2,1,0:T(8,128)(2,1)S(1)} all-to-all(bf16[64,24,896]{2,1,0:T(8,128)(2,1)S(1)} %bitcast.11), channel_id=1, replica_groups=mesh['z'=4,'x'=4,'y'=4,'c'=2] {'y','z','x'}, dimensions={0} | all-to-all | bytes 5505024 | tf_op jit(solution)/shard_map/all_to_all | solution.py:177
  113.1 1.2 %combine.1 = bf16[8,7168]{1,0:T(8,128)(2,1)} custom-call(bf16[64,768]{1,0:T(8,128)(2,1)S(1)} %get-tuple-element.12.mix_ref, bf16[4,384,896]{2,1,0:T(8,128)(2,1)S(1)} %bitcast.10), custom_call_target="tpu_custom_call" | custom-call | tf_op jit(solution)/shard_map/combine/pallas_call | solution.py:63
  (13 shorter events, 0.0 us)
Async XLA Ops:
  0.6 54.2 %copy-start = (bf16[2,128,576]{1,2,0:T(8,128)(2,1)S(1)}, bf16[2,128,576]{1,2,0:T(8,128)(2,1)}, u32[]{:S(2)}) copy-start(bf16[2,128,576]{1,2,0:T(8,128)(2,1)} %param.9) | copy-start | bytes 884740
  0.6 65.6 %collective-permute-start.2 = (bf16[512,7168]{1,0:T(8,128)(2,1)}, bf16[512,7168]{1,0:T(8,128)(2,1)S(1)}, u32[]{:S(2)}, u32[]{:S(2)}) collective-permute-start(bf16[512,7168]{1,0:T(8,128)(2,1)} %own_down.1), channel_id=1, source_target_pairs={{0,1},{1,0},{2,3},{3,2},{4,5},{5,4},{6,7},{7,6},{8,9},{9,8},{10,11... | collective-permute-start | bytes 22020104 | tf_op jit(solution)/shard_map/ppermute | solution.py:181
  0.7 0.9 copy-start.1
  1.6 0.7 copy-start.2
  2.3 0.7 copy-start.3
  4.0 55.7 %slice-start = ((s8[7340032]{0:T(1024)(128)(4,1)}), s8[4194304]{0:T(1024)(128)(4,1)S(1)}, s32[]{:S(2)}) async-start(s8[7340032]{0:T(1024)(128)(4,1)} %bitcast.6), calls=%async_computation.2 | async-start | bytes 8388608
  4.1 55.7 %slice-start.2 = ((s8[7340032]{0:T(1024)(128)(4,1)}), s8[4194304]{0:T(1024)(128)(4,1)S(1)}, s32[]{:S(2)}) async-start(s8[7340032]{0:T(1024)(128)(4,1)} %bitcast.8), calls=%async_computation.4 | async-start | bytes 8388608
  53.6 1.1 copy-start.5
  53.6 1.7 %copy-start.4 = (bf16[2,1024,576]{1,2,0:T(8,128)(2,1)S(1)}, bf16[2,1024,576]{1,2,0:T(8,128)(2,1)}, u32[]{:S(2)}) copy-start(bf16[2,1024,576]{1,2,0:T(8,128)(2,1)} %param.10) | copy-start | bytes 7077892
  53.6 6.2 %slice-start.1 = ((s8[7340032]{0:T(1024)(128)(4,1)}), s8[3145728]{0:T(1024)(128)(4,1)S(1)}, s32[]{:S(2)}) async-start(s8[7340032]{0:T(1024)(128)(4,1)} %bitcast.6), calls=%async_computation.3 | async-start | bytes 6291456
  53.6 6.2 %slice-start.3 = ((s8[7340032]{0:T(1024)(128)(4,1)}), s8[3145728]{0:T(1024)(128)(4,1)S(1)}, s32[]{:S(2)}) async-start(s8[7340032]{0:T(1024)(128)(4,1)} %bitcast.8), calls=%async_computation.5 | async-start | bytes 6291456
  54.6 5.2 %collective-permute-start = (bf16[192,7168]{1,0:T(8,128)(2,1)S(1)}, bf16[192,7168]{1,0:T(8,128)(2,1)S(1)}, u32[]{:S(2)}, u32[]{:S(2)}) collective-permute-start(bf16[192,7168]{1,0:T(8,128)(2,1)S(1)} %unfold.1.rows_ref), channel_id=1, source_target_pairs={{0,1},{1,0},{2,3},{3,2},{4,5},{5,4},{6,7},{7,6},{8,9},{9,8},{10,11... | collective-permute-start | bytes 8257544 | tf_op jit(solution)/shard_map/ppermute | solution.py:181
  59.8 6.5 %slice-start.4 = ((s8[7340032]{0:T(1024)(128)(4,1)}), s8[4194304]{0:T(1024)(128)(4,1)S(1)}, s32[]{:S(2)}) async-start(s8[7340032]{0:T(1024)(128)(4,1)} %bitcast.12), calls=%async_computation.6 | async-start | bytes 8388608
  62.8 3.5 %slice-start.5 = ((s8[7340032]{0:T(1024)(128)(4,1)}), s8[3145728]{0:T(1024)(128)(4,1)S(1)}, s32[]{:S(2)}) async-start(s8[7340032]{0:T(1024)(128)(4,1)} %bitcast.12), calls=%async_computation.7 | async-start | bytes 6291456
  62.9 3.4 %collective-permute-start.1 = (bf16[192,512]{1,0:T(8,128)(2,1)S(1)}, bf16[192,512]{1,0:T(8,128)(2,1)S(1)}, u32[]{:S(2)}, u32[]{:S(2)}) collective-permute-start(bf16[192,512]{1,0:T(8,128)(2,1)S(1)} %hidden.3), channel_id=1, source_target_pairs={{0,1},{1,0},{2,3},{3,2},{4,5},{5,4},{6,7},{7,6},{8,9},{9,8},{10,11... | collective-permute-start | bytes 589832 | tf_op jit(solution)/shard_map/ppermute | solution.py:181

commit v3 on v2

--- a/solution.py
+++ b/solution.py
@@ -14,6 +14,7 @@
 D = 7168
 HIDDEN = 512
 ROWS = 8
+META = 128
 FOLD = 8
 WIDTH = D // FOLD
 CELLS = 16
@@ -97,8 +98,9 @@
     return lanes, place, same_part
 
 
-def select_kernel(input_ref, ids_ref, gates_ref, send_ref, mix_ref):
-    ids, gates = ids_ref[...].astype(F32), gates_ref[...].astype(F32)
+def select_kernel(input_ref, send_ref, mix_ref):
+    meta = input_ref[:, D:].astype(F32)
+    ids, gates = meta[:, :TOP], meta[:, TOP : 2 * TOP]
     lane = index_of((ROWS, EXPERTS), 1)
     member = jnp.zeros(lane.shape, F32)
     gate = jnp.zeros(lane.shape, F32)
@@ -149,10 +151,11 @@
 
 
 def down_kernel(own_ref, other_ref, own_down, other_down, made_ref, parts):
-    for k in range(FOLD):
-        columns = slice(k * WIDTH, (k + 1) * WIDTH)
+    for k in range(0, FOLD, 2):
+        columns = slice(k * WIDTH, (k + 2) * WIDTH)
         made = dot(own_ref[...], own_down[:, columns]) + dot(other_ref[...], other_down[:, columns])
-        parts[k] = made.astype(BF16)
+        made = made.astype(BF16)
+        parts[k], parts[k + 1] = made[:, :WIDTH], made[:, WIDTH:]
     row, column = index_of((TILE, TILE), 0), index_of((TILE, TILE), 1)
     order = remainder(row, FOLD) * CHUNK + quotient(row, FOLD) == column
     order = jnp.where(order, 1.0, 0.0).astype(BF16)
@@ -188,33 +191,39 @@
 def expert_rows(
     attention, expert_input, expert_ids, route_gates, gate_weight, up_weight, down_weight
 ):
+    ids = jnp.pad(expert_ids.astype(BF16), ((0, 0), (D, META - TOP)))
+    gates = jnp.pad(route_gates, ((0, 0), (D + TOP, META - 2 * TOP)))
+    packed = jnp.pad(expert_input, ((0, 0), (0, META)))
+    packed = packed + (ids + gates)
     send, mix = call(
         select_kernel, "select",
         (array(2, 2, CELLS * MESSAGE, WIDTH), array(FOLD * ROWS, 2 * CELLS * MESSAGE)),
-        expert_input, expert_ids, route_gates,
+        packed, cost_estimate=cost(8 * 10**9, 4 * SLOTS * D),
     )
     got = exchange(send).reshape(SLOTS * FOLD, WIDTH)
     down_other = swap_cores(down_weight)
     rows = call(
-        unfold_kernel, "unfold", array(SLOTS, D), got, cost_estimate=cost(8 * 10**9, 4 * SLOTS * D)
+        unfold_kernel, "unfold", array(SLOTS, D), got, cost_estimate=cost(10**9, 4 * SLOTS * D)
     )
     rows_other = swap_cores(rows)
     queries, latent_cache, cache_lengths = attention
     queries, rows = lax.optimization_barrier((queries, rows))
     context = attention_rows(queries, latent_cache, cache_lengths)
-    context, rows = lax.optimization_barrier((context, rows))
 
     flops, size = 4 * SLOTS * D * HIDDEN, 4 * D * HIDDEN
-    own, other = (
-        call(
+
+    def hidden_rows(held):
+        return call(
             hidden_kernel, "hidden", array(SLOTS, HIDDEN), held, gate_weight, up_weight,
             cost_estimate=cost(flops, size),
         )
-        for held in (rows, rows_other)
-    )
+
+    own, rows_other = lax.optimization_barrier((hidden_rows(rows), rows_other))
+    other = swap_cores(hidden_rows(rows_other))
+    context, other = lax.optimization_barrier((context, other))
     made = call(
         down_kernel, "down", array(SLOTS * FOLD, WIDTH),
-        own, swap_cores(other), down_weight, down_other, cost_estimate=cost(flops, size),
+        own, other, down_weight, down_other, cost_estimate=cost(flops, size),
         scratch_shapes=[pltpu.VMEM((FOLD, SLOTS, WIDTH), BF16)],
     )
     returned = exchange(made).reshape(4, CELLS * MESSAGE, WIDTH)

time: 115 us -> 112 us (0.974)
  local copies, waits for them, and re-layouts: 2.81 us -> 0.04 us
  other arithmetic: 0.61 us -> 2.29 us
    unnamed x24 -> x14, local copies, waits for them, and re-layouts: 2.81 us -> 0.04 us
  transfers between devices with their start and end apart: 3 -> 3, of which waited for: 1 -> 1; matrix products, arithmetic and copies ran while one was open for 2% -> 4% of each run, Pallas kernels for 7% -> 7%
where the time goes in v3:
time: 112 us
  blocking collectives  92 us (82%)
  Pallas kernels  13.2 us (12%)
  other arithmetic  2.29 us (2%)
  matrix products  2.19 us (2%)
    all_to_all x2, blocking collectives, exchange(): lax.all_to_all(values, ('y', 'z', 'x'), split_axis=0, concat_axis=0, tile...  92 us
    pallas_call x6, Pallas kernels, call(): pl.pallas_call(kernel, in_specs=[pl.BlockSpec(memory_space=pltpu.SMEM)] *...  13.2 us
  transfers between devices with their start and end apart: 3, of which 1 were waited for; matrix products, arithmetic and copies ran while one was open for 4% of the time, Pallas kernels for 7%

profile of v3, /device:TPU:0, one launch (start us, length us, event | category | flops | bytes accessed | tf_op | source)
XLA Modules:
  0.0 111.8 jit_solution(10027726677553478117)
XLA Ops:
  0.6 0.0 copy-start
  0.6 0.1 collective-permute-start.2
  0.7 0.7 convert_element_type.15
  1.4 1.0 add_add_fusion.input_ref
  2.4 1.0 select.4
  3.5 0.0 copy-start.1
  3.5 49.5 %all_to_all.10 = bf16[64,24,896]{2,1,0:T(8,128)(2,1)S(1)} all-to-all(bf16[64,24,896]{2,1,0:T(8,128)(2,1)S(1)} %bitcast.11), channel_id=1, replica_groups=mesh['z'=4,'x'=4,'y'=4,'c'=2] {'y','z','x'}, dimensions={0} | all-to-all | bytes 5505024 | tf_op jit(solution)/shard_map/all_to_all | solution.py:180
  53.0 1.0 unfold.1.rows_ref
  54.0 0.1 collective-permute-start
  54.1 0.0 copy-done.4
  54.1 0.1 iota_compare_fusion
  54.2 0.0 copy-done.2
  54.2 0.0 copy-done.1
  54.2 0.0 copy-start.3
  54.2 3.0 %hidden.2.own_ref = bf16[192,512]{1,0:T(8,128)(2,1)S(1)} custom-call(bf16[192,7168]{1,0:T(8,128)(2,1)S(1)} %unfold.1.rows_ref, bf16[7168,512]{1,0:T(8,128)(2,1)S(1)} %copy-done.1, bf16[7168,512]{1,0:T(8,128)(2,1)S(1)} %copy-done.2), custom_call_target="tpu_custom_call" | custom-call | flops 2818572288 | bytes 14680064 | tf_op jit(solution)/shard_map/hidden/pallas_call | solution.py:64
  57.2 0.0 copy-done
  57.2 0.0 copy-done.3
  57.2 0.6 convolution_multiply_fusion
  57.9 0.0 slice-start
  57.9 0.5 fusion.18
  58.4 0.0 slice-start.1
  58.5 0.7 collective-permute-done.rows_ref
  59.2 3.0 %hidden.3 = bf16[192,512]{1,0:T(8,128)(2,1)S(1)} custom-call(bf16[192,7168]{1,0:T(8,128)(2,1)S(1)} %collective-permute-done.rows_ref, bf16[7168,512]{1,0:T(8,128)(2,1)S(1)} %copy-done.1, bf16[7168,512]{1,0:T(8,128)(2,1)S(1)} %copy-done.2), custom_call_target="tpu_custom_call" | custom-call | flops 2818572288 | bytes 14680064 | tf_op jit(solution)/shard_map/hidden/pallas_call | solution.py:64
  62.2 0.4 collective-permute-start.1
  62.6 1.5 %fusion.11 = bf16[2,128,512]{2,1,0:T(8,128)(2,1)} fusion(bf16[2,1024,576]{1,2,0:T(8,128)(2,1)S(1)} %copy-done.3, f32[2,128,1024]{2,1,0:T(8,128)S(1)} %get-tuple-element.19, f32[2,128]{1,0:T(2,128)S(1)} %get-tuple-element.18), kind=kOutput, calls=%fused_computation.9 | convolution fusion | flops 269090816 | bytes 3408896 | tf_op jit(solution)/shard_map/rhj,rjl->rhl/dot_general | solution.py:41
  64.1 0.0 collective-permute-done.1.other_ref
  64.1 0.0 collective-permute-done.2.other_down
  64.1 0.0 slice-done
  64.1 0.0 slice-done.1
  64.2 3.9 %down.1 = bf16[1536,896]{1,0:T(8,128)(2,1)S(1)} custom-call(bf16[192,512]{1,0:T(8,128)(2,1)S(1)} %hidden.2.own_ref, bf16[192,512]{1,0:T(8,128)(2,1)S(1)} %collective-permute-done.1.other_ref, bf16[512,7168]{1,0:T(8,128)(2,1)S(1)} %bitcast.10, bf16[512,7168]{1,0:T(8,128)(2,1)S(1)} %collective-permute-done.2.other_down), custom_call_target="tpu_custom_call" | custom-call | flops 2818572288 | bytes 14680064 | tf_op jit(solution)/shard_map/down/pallas_call | solution.py:64
  68.1 42.5 %all_to_all.11 = bf16[64,24,896]{2,1,0:T(8,128)(2,1)S(1)} all-to-all(bf16[64,24,896]{2,1,0:T(8,128)(2,1)S(1)} %bitcast.8), channel_id=1, replica_groups=mesh['z'=4,'x'=4,'y'=4,'c'=2] {'y','z','x'}, dimensions={0} | all-to-all | bytes 5505024 | tf_op jit(solution)/shard_map/all_to_all | solution.py:180
  110.6 1.2 %combine.1 = bf16[8,7168]{1,0:T(8,128)(2,1)} custom-call(bf16[64,768]{1,0:T(8,128)(2,1)S(1)} %get-tuple-element.15.mix_ref, bf16[4,384,896]{2,1,0:T(8,128)(2,1)S(1)} %bitcast.6), custom_call_target="tpu_custom_call" | custom-call | tf_op jit(solution)/shard_map/combine/pallas_call | solution.py:64
  (3 shorter events, 0.0 us)
Async XLA Ops:
  0.6 56.6 %copy-start = (bf16[2,128,576]{1,2,0:T(8,128)(2,1)S(1)}, bf16[2,128,576]{1,2,0:T(8,128)(2,1)}, u32[]{:S(2)}) copy-start(bf16[2,128,576]{1,2,0:T(8,128)(2,1)} %param.9) | copy-start | bytes 884740
  0.6 63.5 %collective-permute-start.2 = (bf16[512,7168]{1,0:T(8,128)(2,1)}, bf16[512,7168]{1,0:T(8,128)(2,1)S(1)}, u32[]{:S(2)}, u32[]{:S(2)}) collective-permute-start(bf16[512,7168]{1,0:T(8,128)(2,1)} %own_down.1), channel_id=1, source_target_pairs={{0,1},{1,0},{2,3},{3,2},{4,5},{5,4},{6,7},{7,6},{8,9},{9,8},{10,11... | collective-permute-start | bytes 22020104 | tf_op jit(solution)/shard_map/ppermute | solution.py:184
  2.4 51.7 %copy-start.2 = (bf16[7168,512]{1,0:T(8,128)(2,1)S(1)}, bf16[7168,512]{1,0:T(8,128)(2,1)}, u32[]{:S(2)}) copy-start(bf16[7168,512]{1,0:T(8,128)(2,1)} %up_ref.3) | copy-start | bytes 22020100
  3.5 50.7 %copy-start.1 = (bf16[7168,512]{1,0:T(8,128)(2,1)S(1)}, bf16[7168,512]{1,0:T(8,128)(2,1)}, u32[]{:S(2)}) copy-start(bf16[7168,512]{1,0:T(8,128)(2,1)} %gate_ref.3) | copy-start | bytes 22020100
  53.0 1.1 copy-start.4
  54.0 5.2 %collective-permute-start = (bf16[192,7168]{1,0:T(8,128)(2,1)S(1)}, bf16[192,7168]{1,0:T(8,128)(2,1)S(1)}, u32[]{:S(2)}, u32[]{:S(2)}) collective-permute-start(bf16[192,7168]{1,0:T(8,128)(2,1)S(1)} %unfold.1.rows_ref), channel_id=1, source_target_pairs={{0,1},{1,0},{2,3},{3,2},{4,5},{5,4},{6,7},{7,6},{8,9},{9,8},{10,11... | collective-permute-start | bytes 8257544 | tf_op jit(solution)/shard_map/ppermute | solution.py:184
  54.2 3.1 %copy-start.3 = (bf16[2,1024,576]{1,2,0:T(8,128)(2,1)S(1)}, bf16[2,1024,576]{1,2,0:T(8,128)(2,1)}, u32[]{:S(2)}) copy-start(bf16[2,1024,576]{1,2,0:T(8,128)(2,1)} %param.10) | copy-start | bytes 7077892
  57.9 6.2 %slice-start = ((s8[7340032]{0:T(1024)(128)(4,1)}), s8[4194304]{0:T(1024)(128)(4,1)S(1)}, s32[]{:S(2)}) async-start(s8[7340032]{0:T(1024)(128)(4,1)} %bitcast.9), calls=%async_computation.2 | async-start | bytes 8388608
  58.4 5.7 %slice-start.1 = ((s8[7340032]{0:T(1024)(128)(4,1)}), s8[3145728]{0:T(1024)(128)(4,1)S(1)}, s32[]{:S(2)}) async-start(s8[7340032]{0:T(1024)(128)(4,1)} %bitcast.9), calls=%async_computation.3 | async-start | bytes 6291456
  62.2 2.0 %collective-permute-start.1 = (bf16[192,512]{1,0:T(8,128)(2,1)S(1)}, bf16[192,512]{1,0:T(8,128)(2,1)S(1)}, u32[]{:S(2)}, u32[]{:S(2)}) collective-permute-start(bf16[192,512]{1,0:T(8,128)(2,1)S(1)} %hidden.3), channel_id=1, source_target_pairs={{0,1},{1,0},{2,3},{3,2},{4,5},{5,4},{6,7},{7,6},{8,9},{9,8},{10,11... | collective-permute-start | bytes 589832 | tf_op jit(solution)/shard_map/ppermute | solution.py:184

commit v4 on v3

--- a/solution.py
+++ b/solution.py
@@ -23,7 +23,7 @@
 SLOTS = SENDERS * CAP
 CHUNK = 32
 TILE = CHUNK * FOLD
-ALL = ("z", "x", "y", "c")
+ALL = "device"
 BF16 = jnp.bfloat16
 F32 = jnp.float32
 
@@ -93,7 +93,7 @@
     lanes = (2 * CELLS * MESSAGE, EXPERTS)
     q = index_of(lanes, 0)
     h = quotient(q, CELLS * MESSAGE)
-    expert = quotient(q - h * (CELLS * MESSAGE), MESSAGE) * 2 + h
+    expert = (EXPERTS - 1) - (quotient(q - h * (CELLS * MESSAGE), MESSAGE) * 2 + h)
     lanes = jnp.where(expert == index_of(lanes, 1), 1.0, 0.0).astype(BF16)
     return lanes, place, same_part
 
@@ -175,13 +175,23 @@
         out_ref[:, k * WIDTH : (k + 1) * WIDTH] = total[k * ROWS : (k + 1) * ROWS]
 
 
+def place_of(z, x, y, c):
+    return ((z * 4 + x) * 4 + y) * 2 + c
+
+
+ORDER = (3, 2, 1, 0)
+SAME_CORE = [[place_of(z, x, y, c) for y in ORDER for z in ORDER for x in ORDER] for c in range(2)]
+
+
 def exchange(values):
     values = values.reshape(SENDERS, MESSAGE, WIDTH)
-    return lax.all_to_all(values, ("y", "z", "x"), split_axis=0, concat_axis=0, tiled=True)
+    return lax.all_to_all(
+        values, ALL, split_axis=0, concat_axis=0, axis_index_groups=SAME_CORE, tiled=True
+    )
 
 
 def swap_cores(values):
-    return lax.ppermute(values, "c", [(0, 1), (1, 0)])
+    return lax.ppermute(values, ALL, [(i, i ^ 1) for i in range(2 * SENDERS)])
 
 
 def cost(flops, size):
@@ -248,7 +258,7 @@
 
 
 def solution(mesh):
-    chips = Mesh(mesh.devices.reshape(4, 4, 4, 2), ALL)
+    chips = Mesh(mesh.devices.reshape(2 * SENDERS), (ALL,))
     return jax.shard_map(
         per_device,
         mesh=chips,

time: 112 us -> 108 us (0.964)
  blocking collectives: 92 us -> 88.5 us
    all_to_all x2, blocking collectives: 92 us -> 88.5 us  [exchange(): lax.all_to_all(values, ALL, split_axis=0, concat_axis=0, axis_index_group...]
where the time goes in v4:
time: 108 us
  blocking collectives  88.5 us (82%)
  Pallas kernels  13.2 us (12%)
  other arithmetic  2.29 us (2%)
  matrix products  2.19 us (2%)
    all_to_all x2, blocking collectives, exchange(): lax.all_to_all(values, ALL, split_axis=0, concat_axis=0, axis_index_group...  88.5 us
    pallas_call x6, Pallas kernels, call(): pl.pallas_call(kernel, in_specs=[pl.BlockSpec(memory_space=pltpu.SMEM)] *...  13.2 us
  transfers between devices with their start and end apart: 3, of which 1 were waited for; matrix products, arithmetic and copies ran while one was open for 4% of the time, Pallas kernels for 7%

profile of v4, /device:TPU:0, one launch (start us, length us, event | category | flops | bytes accessed | tf_op | source)
XLA Modules:
  0.0 108.2 jit_solution(3308978960593403580)
XLA Ops:
  0.6 0.0 copy-start
  0.6 0.1 collective-permute-start.2
  0.7 0.7 convert_element_type.15
  1.4 1.0 add_add_fusion.input_ref
  2.4 1.0 select.4
  3.5 0.0 copy-start.1
  3.5 45.6 %all_to_all.10 = bf16[64,24,896]{2,1,0:T(8,128)(2,1)S(1)} all-to-all(bf16[64,24,896]{2,1,0:T(8,128)(2,1)S(1)} %bitcast.11), channel_id=1, replica_groups={{126,118,110,102,94,86,78,70,62,54,46,38,30,22,14,6,124,116,108,100,92,..., dimensions={0} | all-to-all | bytes 5505024 | tf_op jit(solution)/shard_map/all_to_all | solution.py:188
  49.1 1.0 unfold.1.rows_ref
  50.1 0.1 collective-permute-start
  50.2 0.0 copy-done.4
  50.2 0.1 iota_compare_fusion
  50.3 0.0 copy-done.2
  50.3 0.0 copy-done.1
  50.3 0.0 copy-start.3
  50.3 3.0 %hidden.2.own_ref = bf16[192,512]{1,0:T(8,128)(2,1)S(1)} custom-call(bf16[192,7168]{1,0:T(8,128)(2,1)S(1)} %unfold.1.rows_ref, bf16[7168,512]{1,0:T(8,128)(2,1)S(1)} %copy-done.1, bf16[7168,512]{1,0:T(8,128)(2,1)S(1)} %copy-done.2), custom_call_target="tpu_custom_call" | custom-call | flops 2818572288 | bytes 14680064 | tf_op jit(solution)/shard_map/hidden/pallas_call | solution.py:64
  53.3 0.0 copy-done
  53.3 0.0 copy-done.3
  53.4 0.6 convolution_multiply_fusion
  54.0 0.0 slice-start
  54.0 0.5 fusion.18
  54.6 0.0 slice-start.1
  54.6 0.7 collective-permute-done.rows_ref
  55.3 3.0 %hidden.3 = bf16[192,512]{1,0:T(8,128)(2,1)S(1)} custom-call(bf16[192,7168]{1,0:T(8,128)(2,1)S(1)} %collective-permute-done.rows_ref, bf16[7168,512]{1,0:T(8,128)(2,1)S(1)} %copy-done.1, bf16[7168,512]{1,0:T(8,128)(2,1)S(1)} %copy-done.2), custom_call_target="tpu_custom_call" | custom-call | flops 2818572288 | bytes 14680064 | tf_op jit(solution)/shard_map/hidden/pallas_call | solution.py:64
  58.3 0.4 collective-permute-start.1
  58.7 1.6 %fusion.11 = bf16[2,128,512]{2,1,0:T(8,128)(2,1)} fusion(bf16[2,1024,576]{1,2,0:T(8,128)(2,1)S(1)} %copy-done.3, f32[2,128,1024]{2,1,0:T(8,128)S(1)} %get-tuple-element.19, f32[2,128]{1,0:T(2,128)S(1)} %get-tuple-element.18), kind=kOutput, calls=%fused_computation.9 | convolution fusion | flops 269090816 | bytes 3408896 | tf_op jit(solution)/shard_map/rhj,rjl->rhl/dot_general | solution.py:41
  60.3 0.0 collective-permute-done.1.other_ref
  60.3 0.0 collective-permute-done.2.other_down
  60.3 0.0 slice-done
  60.3 0.0 slice-done.1
  60.3 3.9 %down.1 = bf16[1536,896]{1,0:T(8,128)(2,1)S(1)} custom-call(bf16[192,512]{1,0:T(8,128)(2,1)S(1)} %hidden.2.own_ref, bf16[192,512]{1,0:T(8,128)(2,1)S(1)} %collective-permute-done.1.other_ref, bf16[512,7168]{1,0:T(8,128)(2,1)S(1)} %bitcast.10, bf16[512,7168]{1,0:T(8,128)(2,1)S(1)} %collective-permute-done.2.other_down), custom_call_target="tpu_custom_call" | custom-call | flops 2818572288 | bytes 14680064 | tf_op jit(solution)/shard_map/down/pallas_call | solution.py:64
  64.2 42.8 %all_to_all.11 = bf16[64,24,896]{2,1,0:T(8,128)(2,1)S(1)} all-to-all(bf16[64,24,896]{2,1,0:T(8,128)(2,1)S(1)} %bitcast.8), channel_id=1, replica_groups={{126,118,110,102,94,86,78,70,62,54,46,38,30,22,14,6,124,116,108,100,92,..., dimensions={0} | all-to-all | bytes 5505024 | tf_op jit(solution)/shard_map/all_to_all | solution.py:188
  107.0 1.2 %combine.1 = bf16[8,7168]{1,0:T(8,128)(2,1)} custom-call(bf16[64,768]{1,0:T(8,128)(2,1)S(1)} %get-tuple-element.15.mix_ref, bf16[4,384,896]{2,1,0:T(8,128)(2,1)S(1)} %bitcast.6), custom_call_target="tpu_custom_call" | custom-call | tf_op jit(solution)/shard_map/combine/pallas_call | solution.py:64
  (3 shorter events, 0.0 us)
Async XLA Ops:
  0.6 52.7 %copy-start = (bf16[2,128,576]{1,2,0:T(8,128)(2,1)S(1)}, bf16[2,128,576]{1,2,0:T(8,128)(2,1)}, u32[]{:S(2)}) copy-start(bf16[2,128,576]{1,2,0:T(8,128)(2,1)} %param.9) | copy-start | bytes 884740
  0.6 59.6 %collective-permute-start.2 = (bf16[512,7168]{1,0:T(8,128)(2,1)}, bf16[512,7168]{1,0:T(8,128)(2,1)S(1)}, u32[]{:S(2)}, u32[]{:S(2)}) collective-permute-start(bf16[512,7168]{1,0:T(8,128)(2,1)} %own_down.1), channel_id=1, source_target_pairs={{0,1},{1,0},{2,3},{3,2},{4,5},{5,4},{6,7},{7,6},{8,9},{9,8},{10,11... | collective-permute-start | bytes 22020104 | tf_op jit(solution)/shard_map/ppermute | solution.py:194
  2.4 47.9 %copy-start.2 = (bf16[7168,512]{1,0:T(8,128)(2,1)S(1)}, bf16[7168,512]{1,0:T(8,128)(2,1)}, u32[]{:S(2)}) copy-start(bf16[7168,512]{1,0:T(8,128)(2,1)} %up_ref.3) | copy-start | bytes 22020100
  3.5 46.8 %copy-start.1 = (bf16[7168,512]{1,0:T(8,128)(2,1)S(1)}, bf16[7168,512]{1,0:T(8,128)(2,1)}, u32[]{:S(2)}) copy-start(bf16[7168,512]{1,0:T(8,128)(2,1)} %gate_ref.3) | copy-start | bytes 22020100
  49.1 1.1 %copy-start.4 = (s32[2]{0:T(128)S(1)}, s32[2]{0:T(128)}, u32[]{:S(2)}) copy-start(s32[2]{0:T(128)} %param.11) | copy-start | bytes 28
  50.1 5.2 %collective-permute-start = (bf16[192,7168]{1,0:T(8,128)(2,1)S(1)}, bf16[192,7168]{1,0:T(8,128)(2,1)S(1)}, u32[]{:S(2)}, u32[]{:S(2)}) collective-permute-start(bf16[192,7168]{1,0:T(8,128)(2,1)S(1)} %unfold.1.rows_ref), channel_id=1, source_target_pairs={{0,1},{1,0},{2,3},{3,2},{4,5},{5,4},{6,7},{7,6},{8,9},{9,8},{10,11... | collective-permute-start | bytes 8257544 | tf_op jit(solution)/shard_map/ppermute | solution.py:194
  50.3 3.0 %copy-start.3 = (bf16[2,1024,576]{1,2,0:T(8,128)(2,1)S(1)}, bf16[2,1024,576]{1,2,0:T(8,128)(2,1)}, u32[]{:S(2)}) copy-start(bf16[2,1024,576]{1,2,0:T(8,128)(2,1)} %param.10) | copy-start | bytes 7077892
  54.0 6.3 %slice-start = ((s8[7340032]{0:T(1024)(128)(4,1)}), s8[4194304]{0:T(1024)(128)(4,1)S(1)}, s32[]{:S(2)}) async-start(s8[7340032]{0:T(1024)(128)(4,1)} %bitcast.9), calls=%async_computation.2 | async-start | bytes 8388608
  54.6 5.7 %slice-start.1 = ((s8[7340032]{0:T(1024)(128)(4,1)}), s8[3145728]{0:T(1024)(128)(4,1)S(1)}, s32[]{:S(2)}) async-start(s8[7340032]{0:T(1024)(128)(4,1)} %bitcast.9), calls=%async_computation.3 | async-start | bytes 6291456
  58.3 1.9 %collective-permute-start.1 = (bf16[192,512]{1,0:T(8,128)(2,1)S(1)}, bf16[192,512]{1,0:T(8,128)(2,1)S(1)}, u32[]{:S(2)}, u32[]{:S(2)}) collective-permute-start(bf16[192,512]{1,0:T(8,128)(2,1)S(1)} %hidden.3), channel_id=1, source_target_pairs={{0,1},{1,0},{2,3},{3,2},{4,5},{5,4},{6,7},{7,6},{8,9},{9,8},{10,11... | collective-permute-start | bytes 589832 | tf_op jit(solution)/shard_map/ppermute | solution.py:194

commit v5 on v4

--- a/solution.py
+++ b/solution.py
@@ -14,7 +14,6 @@
 D = 7168
 HIDDEN = 512
 ROWS = 8
-META = 128
 FOLD = 8
 WIDTH = D // FOLD
 CELLS = 16
@@ -86,21 +85,25 @@
     return values - quotient(values, divisor) * divisor
 
 
-def slot_matches(shape, axis):
+def wanted_places(shape, axis):
     q, p = index_of(shape, axis), index_of(shape, 1 - axis)
     place = quotient(remainder(q, MESSAGE), FOLD)
-    same_part = remainder(q, FOLD) == quotient(p, ROWS)
-    lanes = (2 * CELLS * MESSAGE, EXPERTS)
-    q = index_of(lanes, 0)
+    return jnp.where(remainder(q, FOLD) == quotient(p, ROWS), place, -2.0)
+
+
+def tables_kernel(lanes_ref, wanted_ref, wanted_t_ref):
+    q = index_of(lanes_ref.shape, 0)
     h = quotient(q, CELLS * MESSAGE)
     expert = (EXPERTS - 1) - (quotient(q - h * (CELLS * MESSAGE), MESSAGE) * 2 + h)
-    lanes = jnp.where(expert == index_of(lanes, 1), 1.0, 0.0).astype(BF16)
-    return lanes, place, same_part
-
-
-def select_kernel(input_ref, send_ref, mix_ref):
-    meta = input_ref[:, D:].astype(F32)
-    ids, gates = meta[:, :TOP], meta[:, TOP : 2 * TOP]
+    lanes_ref[...] = jnp.where(expert == index_of(lanes_ref.shape, 1), 1.0, 0.0).astype(BF16)
+    wanted_ref[...] = wanted_places(wanted_ref.shape, 0)
+    wanted_t_ref[...] = wanted_places(wanted_t_ref.shape, 1)
+
+
+def select_kernel(
+    input_ref, ids_ref, gates_ref, lanes_ref, wanted_ref, wanted_t_ref, send_ref, mix_ref
+):
+    ids, gates = ids_ref[...].astype(F32), gates_ref[...].astype(F32)
     lane = index_of((ROWS, EXPERTS), 1)
     member = jnp.zeros(lane.shape, F32)
     gate = jnp.zeros(lane.shape, F32)
@@ -117,17 +120,15 @@
         [input_ref[:, k * WIDTH : (k + 1) * WIDTH] for k in range(FOLD)], axis=0
     )
     half = CELLS * MESSAGE
-
-    lanes, wanted, same_part = slot_matches((2 * half, FOLD * ROWS), 0)
-    chosen = (dot(lanes, place, ((1,), (1,))) == wanted) & same_part
+    lanes = lanes_ref[...]
+    chosen = dot(lanes, place, ((1,), (1,))) == wanted_ref[...]
     pick = jnp.where(chosen, 1.0, 0.0).astype(BF16)
     for h in range(2):
         picked = dot(pick[h * half : (h + 1) * half], folded).astype(BF16)
         send_ref[h, 0] = picked
         send_ref[h, 1] = picked
 
-    _, wanted, same_part = slot_matches((FOLD * ROWS, 2 * half), 1)
-    chosen = (dot(place, lanes, ((1,), (1,))) == wanted) & same_part
+    chosen = dot(place, lanes, ((1,), (1,))) == wanted_t_ref[...]
     weight = dot(gate, lanes, ((1,), (1,)))
     mix_ref[...] = jnp.where(chosen, weight, 0.0).astype(BF16)
 
@@ -201,14 +202,16 @@
 def expert_rows(
     attention, expert_input, expert_ids, route_gates, gate_weight, up_weight, down_weight
 ):
-    ids = jnp.pad(expert_ids.astype(BF16), ((0, 0), (D, META - TOP)))
-    gates = jnp.pad(route_gates, ((0, 0), (D + TOP, META - 2 * TOP)))
-    packed = jnp.pad(expert_input, ((0, 0), (0, META)))
-    packed = packed + (ids + gates)
+    slots, shared = 2 * CELLS * MESSAGE, FOLD * ROWS
+    tables = call(
+        tables_kernel, "tables",
+        (array(slots, EXPERTS), array(slots, shared, dtype=F32), array(shared, slots, dtype=F32)),
+        cost_estimate=cost(8 * 10**9, 4 * SLOTS * D),
+    )
     send, mix = call(
-        select_kernel, "select",
-        (array(2, 2, CELLS * MESSAGE, WIDTH), array(FOLD * ROWS, 2 * CELLS * MESSAGE)),
-        packed, cost_estimate=cost(8 * 10**9, 4 * SLOTS * D),
+        select_kernel, "select", (array(2, 2, CELLS * MESSAGE, WIDTH), array(shared, slots)),
+        expert_input, expert_ids, route_gates, *tables,
+        cost_estimate=cost(8 * 10**9, 4 * SLOTS * D),
     )
     got = exchange(send).reshape(SLOTS * FOLD, WIDTH)
     down_other = swap_cores(down_weight)

time: 108 us -> 107 us (level)
  other arithmetic: 2.29 us -> 0.61 us
    pallas_call x6 -> x7, Pallas kernels: 13.2 us -> 13.5 us  [call(): pl.pallas_call(kernel, in_specs=[pl.BlockSpec(memory_space=pltpu.SMEM)] *...]
  transfers between devices with their start and end apart: 3 -> 3, of which waited for: 1 -> 1; matrix products, arithmetic and copies ran while one was open for 4% -> 3% of each run, Pallas kernels for 7% -> 8%
where the time goes in v5:
time: 107 us; the launch traced here: 106 us
  blocking collectives  87.6 us (82%)
  Pallas kernels  13.5 us (13%)
  matrix products  2.19 us (2%)
    all_to_all x2, blocking collectives, exchange(): lax.all_to_all(values, ALL, split_axis=0, concat_axis=0, axis_index_group...  87.6 us
    pallas_call x7, Pallas kernels, call(): pl.pallas_call(kernel, in_specs=[pl.BlockSpec(memory_space=pltpu.SMEM)] *...  13.5 us
  transfers between devices with their start and end apart: 3, of which 1 were waited for; matrix products, arithmetic and copies ran while one was open for 3% of the time, Pallas kernels for 8%

profile of v5, /device:TPU:0, one launch (start us, length us, event | category | flops | bytes accessed | tf_op | source)
XLA Modules:
  0.0 106.5 jit_solution(3869396651317937813)
XLA Ops:
  0.6 0.0 copy-start
  0.6 0.0 copy-start.3
  0.7 0.0 copy-start.2
  0.7 0.0 copy-start.1
  0.7 0.1 collective-permute-start.2
  0.8 0.0 slice-start
  0.8 0.0 slice-start.2
  0.8 0.4 tables.1
  1.2 0.1 copy-done.3
  1.4 0.0 copy-done.2
  1.4 0.2 copy-done.1
  1.6 1.0 select.1
  2.6 45.2 %all_to_all.10 = bf16[64,24,896]{2,1,0:T(8,128)(2,1)S(1)} all-to-all(bf16[64,24,896]{2,1,0:T(8,128)(2,1)S(1)} %bitcast.15), channel_id=1, replica_groups={{126,118,110,102,94,86,78,70,62,54,46,38,30,22,14,6,124,116,108,100,92,..., dimensions={0} | all-to-all | bytes 5505024 | tf_op jit(solution)/shard_map/all_to_all | solution.py:189
  47.8 1.0 unfold.1.rows_ref
  48.8 0.1 collective-permute-start
  48.9 0.0 copy-done.5
  48.9 0.1 iota_compare_fusion
  49.0 0.0 copy-start.4
  49.0 3.0 %hidden.2.own_ref = bf16[192,512]{1,0:T(8,128)(2,1)S(1)} custom-call(bf16[192,7168]{1,0:T(8,128)(2,1)S(1)} %unfold.1.rows_ref, bf16[7168,512]{1,0:T(8,128)(2,1)S(1)} %bitcast.7, bf16[7168,512]{1,0:T(8,128)(2,1)S(1)} %bitcast.9), custom_call_target="tpu_custom_call" | custom-call | flops 2818572288 | bytes 14680064 | tf_op jit(solution)/shard_map/hidden/pallas_call | solution.py:63
  52.1 0.6 convolution_multiply_fusion
  52.7 0.0 slice-start.4
  52.7 0.5 fusion.18
  53.3 0.0 slice-start.5
  53.3 0.7 collective-permute-done.rows_ref
  54.0 3.0 %hidden.3 = bf16[192,512]{1,0:T(8,128)(2,1)S(1)} custom-call(bf16[192,7168]{1,0:T(8,128)(2,1)S(1)} %collective-permute-done.rows_ref, bf16[7168,512]{1,0:T(8,128)(2,1)S(1)} %bitcast.7, bf16[7168,512]{1,0:T(8,128)(2,1)S(1)} %bitcast.9), custom_call_target="tpu_custom_call" | custom-call | flops 2818572288 | bytes 14680064 | tf_op jit(solution)/shard_map/hidden/pallas_call | solution.py:63
  57.0 0.4 collective-permute-start.1
  57.4 1.5 %fusion.11 = bf16[2,128,512]{2,1,0:T(8,128)(2,1)} fusion(bf16[2,1024,576]{1,2,0:T(8,128)(2,1)S(1)} %copy-done.4, f32[2,128,1024]{2,1,0:T(8,128)S(1)} %get-tuple-element.25, f32[2,128]{1,0:T(2,128)S(1)} %get-tuple-element.24), kind=kOutput, calls=%fused_computation.9 | convolution fusion | flops 269090816 | bytes 3408896 | tf_op jit(solution)/shard_map/rhj,rjl->rhl/dot_general | solution.py:40
  58.9 0.0 collective-permute-done.1.other_ref
  59.0 0.0 collective-permute-done.2.other_down
  59.0 3.9 %down.1 = bf16[1536,896]{1,0:T(8,128)(2,1)S(1)} custom-call(bf16[192,512]{1,0:T(8,128)(2,1)S(1)} %hidden.2.own_ref, bf16[192,512]{1,0:T(8,128)(2,1)S(1)} %collective-permute-done.1.other_ref, bf16[512,7168]{1,0:T(8,128)(2,1)S(1)} %bitcast.14, bf16[512,7168]{1,0:T(8,128)(2,1)S(1)} %collective-permute-done.2.other_down), custom_call_target="tpu_custom_call" | custom-call | flops 2818572288 | bytes 14680064 | tf_op jit(solution)/shard_map/down/pallas_call | solution.py:63
  62.9 42.4 %all_to_all.11 = bf16[64,24,896]{2,1,0:T(8,128)(2,1)S(1)} all-to-all(bf16[64,24,896]{2,1,0:T(8,128)(2,1)S(1)} %bitcast.12), channel_id=1, replica_groups={{126,118,110,102,94,86,78,70,62,54,46,38,30,22,14,6,124,116,108,100,92,..., dimensions={0} | all-to-all | bytes 5505024 | tf_op jit(solution)/shard_map/all_to_all | solution.py:189
  105.3 1.2 %combine.1 = bf16[8,7168]{1,0:T(8,128)(2,1)} custom-call(bf16[64,768]{1,0:T(8,128)(2,1)S(1)} %get-tuple-element.21.mix_ref, bf16[4,384,896]{2,1,0:T(8,128)(2,1)S(1)} %bitcast.10), custom_call_target="tpu_custom_call" | custom-call | tf_op jit(solution)/shard_map/combine/pallas_call | solution.py:63
  (14 shorter events, 0.0 us)
Async XLA Ops:
  0.6 51.4 %copy-start = (bf16[2,128,576]{1,2,0:T(8,128)(2,1)S(1)}, bf16[2,128,576]{1,2,0:T(8,128)(2,1)}, u32[]{:S(2)}) copy-start(bf16[2,128,576]{1,2,0:T(8,128)(2,1)} %param.9) | copy-start | bytes 884740
  0.6 0.7 copy-start.3
  0.7 0.7 copy-start.2
  0.7 1.0 copy-start.1
  0.7 58.3 %collective-permute-start.2 = (bf16[512,7168]{1,0:T(8,128)(2,1)}, bf16[512,7168]{1,0:T(8,128)(2,1)S(1)}, u32[]{:S(2)}, u32[]{:S(2)}) collective-permute-start(bf16[512,7168]{1,0:T(8,128)(2,1)} %own_down.1), channel_id=1, source_target_pairs={{0,1},{1,0},{2,3},{3,2},{4,5},{5,4},{6,7},{7,6},{8,9},{9,8},{10,11... | collective-permute-start | bytes 22020104 | tf_op jit(solution)/shard_map/ppermute | solution.py:195
  0.8 48.2 %slice-start = ((s8[7340032]{0:T(1024)(128)(4,1)}), s8[4194304]{0:T(1024)(128)(4,1)S(1)}, s32[]{:S(2)}) async-start(s8[7340032]{0:T(1024)(128)(4,1)} %bitcast.6), calls=%async_computation.2 | async-start | bytes 8388608
  0.8 48.2 %slice-start.2 = ((s8[7340032]{0:T(1024)(128)(4,1)}), s8[4194304]{0:T(1024)(128)(4,1)S(1)}, s32[]{:S(2)}) async-start(s8[7340032]{0:T(1024)(128)(4,1)} %bitcast.8), calls=%async_computation.4 | async-start | bytes 8388608
  1.6 47.4 %slice-start.1 = ((s8[7340032]{0:T(1024)(128)(4,1)}), s8[3145728]{0:T(1024)(128)(4,1)S(1)}, s32[]{:S(2)}) async-start(s8[7340032]{0:T(1024)(128)(4,1)} %bitcast.6), calls=%async_computation.3 | async-start | bytes 6291456
  1.6 47.4 %slice-start.3 = ((s8[7340032]{0:T(1024)(128)(4,1)}), s8[3145728]{0:T(1024)(128)(4,1)S(1)}, s32[]{:S(2)}) async-start(s8[7340032]{0:T(1024)(128)(4,1)} %bitcast.8), calls=%async_computation.5 | async-start | bytes 6291456
  47.8 1.1 %copy-start.5 = (s32[2]{0:T(128)S(1)}, s32[2]{0:T(128)}, u32[]{:S(2)}) copy-start(s32[2]{0:T(128)} %param.11) | copy-start | bytes 28
  48.8 5.2 %collective-permute-start = (bf16[192,7168]{1,0:T(8,128)(2,1)S(1)}, bf16[192,7168]{1,0:T(8,128)(2,1)S(1)}, u32[]{:S(2)}, u32[]{:S(2)}) collective-permute-start(bf16[192,7168]{1,0:T(8,128)(2,1)S(1)} %unfold.1.rows_ref), channel_id=1, source_target_pairs={{0,1},{1,0},{2,3},{3,2},{4,5},{5,4},{6,7},{7,6},{8,9},{9,8},{10,11... | collective-permute-start | bytes 8257544 | tf_op jit(solution)/shard_map/ppermute | solution.py:195
  49.0 3.0 %copy-start.4 = (bf16[2,1024,576]{1,2,0:T(8,128)(2,1)S(1)}, bf16[2,1024,576]{1,2,0:T(8,128)(2,1)}, u32[]{:S(2)}) copy-start(bf16[2,1024,576]{1,2,0:T(8,128)(2,1)} %param.10) | copy-start | bytes 7077892
  52.7 6.2 %slice-start.4 = ((s8[7340032]{0:T(1024)(128)(4,1)}), s8[4194304]{0:T(1024)(128)(4,1)S(1)}, s32[]{:S(2)}) async-start(s8[7340032]{0:T(1024)(128)(4,1)} %bitcast.13), calls=%async_computation.6 | async-start | bytes 8388608
  53.3 5.7 %slice-start.5 = ((s8[7340032]{0:T(1024)(128)(4,1)}), s8[3145728]{0:T(1024)(128)(4,1)S(1)}, s32[]{:S(2)}) async-start(s8[7340032]{0:T(1024)(128)(4,1)} %bitcast.13), calls=%async_computation.7 | async-start | bytes 6291456
  57.0 1.9 %collective-permute-start.1 = (bf16[192,512]{1,0:T(8,128)(2,1)S(1)}, bf16[192,512]{1,0:T(8,128)(2,1)S(1)}, u32[]{:S(2)}, u32[]{:S(2)}) collective-permute-start(bf16[192,512]{1,0:T(8,128)(2,1)S(1)} %hidden.3), channel_id=1, source_target_pairs={{0,1},{1,0},{2,3},{3,2},{4,5},{5,4},{6,7},{7,6},{8,9},{9,8},{10,11... | collective-permute-start | bytes 589832 | tf_op jit(solution)/shard_map/ppermute | solution.py:195

commit v6 on v5

--- a/solution.py
+++ b/solution.py
@@ -133,7 +133,7 @@
     mix_ref[...] = jnp.where(chosen, weight, 0.0).astype(BF16)
 
 
-def unfold_kernel(got_ref, rows_ref):
+def unfold(got_ref, rows_ref):
     row, column = index_of((TILE, TILE), 0), index_of((TILE, TILE), 1)
     order = remainder(row, CHUNK) * FOLD + quotient(row, CHUNK) == column
     order = jnp.where(order, 1.0, 0.0).astype(BF16)
@@ -145,9 +145,10 @@
             ]
 
 
-def hidden_kernel(rows_ref, gate_ref, up_ref, hidden_ref):
-    gate = dot(rows_ref[...], gate_ref[...])
-    up = dot(rows_ref[...], up_ref[...])
+def hidden_kernel(got_ref, gate_ref, up_ref, hidden_ref, rows):
+    unfold(got_ref, rows)
+    gate = dot(rows[...], gate_ref[...])
+    up = dot(rows[...], up_ref[...])
     hidden_ref[...] = (jax.nn.silu(gate) * up).astype(BF16)
 
 
@@ -215,12 +216,9 @@
     )
     got = exchange(send).reshape(SLOTS * FOLD, WIDTH)
     down_other = swap_cores(down_weight)
-    rows = call(
-        unfold_kernel, "unfold", array(SLOTS, D), got, cost_estimate=cost(10**9, 4 * SLOTS * D)
-    )
-    rows_other = swap_cores(rows)
+    got_other = swap_cores(got)
     queries, latent_cache, cache_lengths = attention
-    queries, rows = lax.optimization_barrier((queries, rows))
+    queries, got = lax.optimization_barrier((queries, got))
     context = attention_rows(queries, latent_cache, cache_lengths)
 
     flops, size = 4 * SLOTS * D * HIDDEN, 4 * D * HIDDEN
@@ -228,11 +226,11 @@
     def hidden_rows(held):
         return call(
             hidden_kernel, "hidden", array(SLOTS, HIDDEN), held, gate_weight, up_weight,
-            cost_estimate=cost(flops, size),
+            cost_estimate=cost(flops, size), scratch_shapes=[pltpu.VMEM((SLOTS, D), BF16)],
         )
 
-    own, rows_other = lax.optimization_barrier((hidden_rows(rows), rows_other))
-    other = swap_cores(hidden_rows(rows_other))
+    own, got_other = lax.optimization_barrier((hidden_rows(got), got_other))
+    other = swap_cores(hidden_rows(got_other))
     context, other = lax.optimization_barrier((context, other))
     made = call(
         down_kernel, "down", array(SLOTS * FOLD, WIDTH),

time: 107 us -> 107 us (level)
    pallas_call x7 -> x6, Pallas kernels: 13.5 us -> 14.2 us  [call(): pl.pallas_call(kernel, in_specs=[pl.BlockSpec(memory_space=pltpu.SMEM)] *...]
  transfers between devices with their start and end apart: 3 -> 3, of which waited for: 1 -> 0; matrix products, arithmetic and copies ran while one was open for 3% -> 3% of each run, Pallas kernels for 8% -> 8%
where the time goes in v6:
time: 107 us; the launch traced here: 106 us
  blocking collectives  87.2 us (81%)
  Pallas kernels  14.2 us (13%)
  matrix products  2.19 us (2%)
    all_to_all x2, blocking collectives, exchange(): lax.all_to_all(values, ALL, split_axis=0, concat_axis=0, axis_index_group...  87.2 us
    pallas_call x6, Pallas kernels, call(): pl.pallas_call(kernel, in_specs=[pl.BlockSpec(memory_space=pltpu.SMEM)] *...  14.2 us
  transfers between devices with their start and end apart: 3, of which 0 were waited for; matrix products, arithmetic and copies ran while one was open for 3% of the time, Pallas kernels for 8%

profile of v6, /device:TPU:0, one launch (start us, length us, event | category | flops | bytes accessed | tf_op | source)
XLA Modules:
  0.0 106.4 jit_solution(17461902887851795854)
XLA Ops:
  0.6 0.0 copy-start
  0.6 0.0 copy-start.3
  0.7 0.0 copy-start.2
  0.7 0.0 copy-start.1
  0.7 0.1 collective-permute-start.2
  0.8 0.4 tables.1
  1.2 0.0 slice-start
  1.2 0.0 slice-start.2
  1.2 0.1 copy-done.3
  1.4 0.0 copy-done.2
  1.4 0.2 copy-done.1
  1.6 1.0 select.1
  2.6 0.0 copy-start.5
  2.6 45.2 %all_to_all.10 = bf16[64,24,896]{2,1,0:T(8,128)(2,1)S(1)} all-to-all(bf16[64,24,896]{2,1,0:T(8,128)(2,1)S(1)} %bitcast.16), channel_id=1, replica_groups={{126,118,110,102,94,86,78,70,62,54,46,38,30,22,14,6,124,116,108,100,92,..., dimensions={0} | all-to-all | bytes 5505024 | tf_op jit(solution)/shard_map/all_to_all | solution.py:190
  47.8 0.0 collective-permute-start
  47.8 0.1 iota_compare_fusion
  47.9 0.0 slice-done.2
  48.0 0.0 copy-start.4
  48.0 3.8 %hidden.2.own_ref = bf16[192,512]{1,0:T(8,128)(2,1)S(1)} custom-call(bf16[1536,896]{1,0:T(8,128)(2,1)S(1)} %bitcast.12, bf16[7168,512]{1,0:T(8,128)(2,1)S(1)} %bitcast.7, bf16[7168,512]{1,0:T(8,128)(2,1)S(1)} %bitcast.9), custom_call_target="tpu_custom_call" | custom-call | flops 2818572288 | bytes 14680064 | tf_op jit(solution)/shard_map/hidden/pallas_call | solution.py:63
  51.8 0.6 convolution_multiply_fusion
  52.5 0.0 slice-start.4
  52.5 0.5 fusion.18
  53.0 0.0 slice-start.5
  53.0 0.0 collective-permute-done.got_ref
  53.0 3.8 %hidden.3 = bf16[192,512]{1,0:T(8,128)(2,1)S(1)} custom-call(bf16[1536,896]{1,0:T(8,128)(2,1)S(1)} %collective-permute-done.got_ref, bf16[7168,512]{1,0:T(8,128)(2,1)S(1)} %bitcast.7, bf16[7168,512]{1,0:T(8,128)(2,1)S(1)} %bitcast.9), custom_call_target="tpu_custom_call" | custom-call | flops 2818572288 | bytes 14680064 | tf_op jit(solution)/shard_map/hidden/pallas_call | solution.py:63
  56.9 0.8 collective-permute-start.1
  57.6 1.5 %fusion.11 = bf16[2,128,512]{2,1,0:T(8,128)(2,1)} fusion(bf16[2,1024,576]{1,2,0:T(8,128)(2,1)S(1)} %copy-done.4, f32[2,128,1024]{2,1,0:T(8,128)S(1)} %get-tuple-element.25, f32[2,128]{1,0:T(2,128)S(1)} %get-tuple-element.24), kind=kOutput, calls=%fused_computation.9 | convolution fusion | flops 269090816 | bytes 3408896 | tf_op jit(solution)/shard_map/rhj,rjl->rhl/dot_general | solution.py:40
  59.2 0.0 collective-permute-done.1.other_ref
  59.2 0.0 collective-permute-done.2.other_down
  59.2 3.9 %down.1 = bf16[1536,896]{1,0:T(8,128)(2,1)S(1)} custom-call(bf16[192,512]{1,0:T(8,128)(2,1)S(1)} %hidden.2.own_ref, bf16[192,512]{1,0:T(8,128)(2,1)S(1)} %collective-permute-done.1.other_ref, bf16[512,7168]{1,0:T(8,128)(2,1)S(1)} %bitcast.15, bf16[512,7168]{1,0:T(8,128)(2,1)S(1)} %collective-permute-done.2.other_down), custom_call_target="tpu_custom_call" | custom-call | flops 2818572288 | bytes 14680064 | tf_op jit(solution)/shard_map/down/pallas_call | solution.py:63
  63.2 42.0 %all_to_all.11 = bf16[64,24,896]{2,1,0:T(8,128)(2,1)S(1)} all-to-all(bf16[64,24,896]{2,1,0:T(8,128)(2,1)S(1)} %bitcast.13), channel_id=1, replica_groups={{126,118,110,102,94,86,78,70,62,54,46,38,30,22,14,6,124,116,108,100,92,..., dimensions={0} | all-to-all | bytes 5505024 | tf_op jit(solution)/shard_map/all_to_all | solution.py:190
  105.2 1.2 %combine.1 = bf16[8,7168]{1,0:T(8,128)(2,1)} custom-call(bf16[64,768]{1,0:T(8,128)(2,1)S(1)} %get-tuple-element.21.mix_ref, bf16[4,384,896]{2,1,0:T(8,128)(2,1)S(1)} %bitcast.10), custom_call_target="tpu_custom_call" | custom-call | tf_op jit(solution)/shard_map/combine/pallas_call | solution.py:63
  (13 shorter events, 0.0 us)
Async XLA Ops:
  0.6 51.2 %copy-start = (bf16[2,128,576]{1,2,0:T(8,128)(2,1)S(1)}, bf16[2,128,576]{1,2,0:T(8,128)(2,1)}, u32[]{:S(2)}) copy-start(bf16[2,128,576]{1,2,0:T(8,128)(2,1)} %param.9) | copy-start | bytes 884740
  0.6 0.7 copy-start.3
  0.7 0.7 copy-start.2
  0.7 1.0 copy-start.1
  0.7 58.5 %collective-permute-start.2 = (bf16[512,7168]{1,0:T(8,128)(2,1)}, bf16[512,7168]{1,0:T(8,128)(2,1)S(1)}, u32[]{:S(2)}, u32[]{:S(2)}) collective-permute-start(bf16[512,7168]{1,0:T(8,128)(2,1)} %own_down.1), channel_id=1, source_target_pairs={{0,1},{1,0},{2,3},{3,2},{4,5},{5,4},{6,7},{7,6},{8,9},{9,8},{10,11... | collective-permute-start | bytes 22020104 | tf_op jit(solution)/shard_map/ppermute | solution.py:196
  1.2 46.7 %slice-start = ((s8[7340032]{0:T(1024)(128)(4,1)}), s8[4194304]{0:T(1024)(128)(4,1)S(1)}, s32[]{:S(2)}) async-start(s8[7340032]{0:T(1024)(128)(4,1)} %bitcast.6), calls=%async_computation.2 | async-start | bytes 8388608
  1.2 46.7 %slice-start.2 = ((s8[7340032]{0:T(1024)(128)(4,1)}), s8[4194304]{0:T(1024)(128)(4,1)S(1)}, s32[]{:S(2)}) async-start(s8[7340032]{0:T(1024)(128)(4,1)} %bitcast.8), calls=%async_computation.4 | async-start | bytes 8388608
  1.6 46.3 %slice-start.1 = ((s8[7340032]{0:T(1024)(128)(4,1)}), s8[3145728]{0:T(1024)(128)(4,1)S(1)}, s32[]{:S(2)}) async-start(s8[7340032]{0:T(1024)(128)(4,1)} %bitcast.6), calls=%async_computation.3 | async-start | bytes 6291456
  1.6 46.3 %slice-start.3 = ((s8[7340032]{0:T(1024)(128)(4,1)}), s8[3145728]{0:T(1024)(128)(4,1)S(1)}, s32[]{:S(2)}) async-start(s8[7340032]{0:T(1024)(128)(4,1)} %bitcast.8), calls=%async_computation.5 | async-start | bytes 6291456
  2.6 45.2 %copy-start.5 = (s32[2]{0:T(128)S(1)}, s32[2]{0:T(128)}, u32[]{:S(2)}) copy-start(s32[2]{0:T(128)} %param.11) | copy-start | bytes 28
  47.8 5.2 %collective-permute-start = (bf16[1536,896]{1,0:T(8,128)(2,1)S(1)}, bf16[1536,896]{1,0:T(8,128)(2,1)S(1)}, u32[]{:S(2)}, u32[]{:S(2)}) collective-permute-start(bf16[1536,896]{1,0:T(8,128)(2,1)S(1)} %bitcast.11), channel_id=1, source_target_pairs={{0,1},{1,0},{2,3},{3,2},{4,5},{5,4},{6,7},{7,6},{8,9},{9,8},{10,11... | collective-permute-start | bytes 8257544 | tf_op jit(solution)/shard_map/ppermute | solution.py:196
  48.0 3.9 %copy-start.4 = (bf16[2,1024,576]{1,2,0:T(8,128)(2,1)S(1)}, bf16[2,1024,576]{1,2,0:T(8,128)(2,1)}, u32[]{:S(2)}) copy-start(bf16[2,1024,576]{1,2,0:T(8,128)(2,1)} %param.10) | copy-start | bytes 7077892
  52.5 6.7 %slice-start.4 = ((s8[7340032]{0:T(1024)(128)(4,1)}), s8[4194304]{0:T(1024)(128)(4,1)S(1)}, s32[]{:S(2)}) async-start(s8[7340032]{0:T(1024)(128)(4,1)} %bitcast.14), calls=%async_computation.6 | async-start | bytes 8388608
  53.0 6.2 %slice-start.5 = ((s8[7340032]{0:T(1024)(128)(4,1)}), s8[3145728]{0:T(1024)(128)(4,1)S(1)}, s32[]{:S(2)}) async-start(s8[7340032]{0:T(1024)(128)(4,1)} %bitcast.14), calls=%async_computation.7 | async-start | bytes 6291456
  56.9 2.3 %collective-permute-start.1 = (bf16[192,512]{1,0:T(8,128)(2,1)S(1)}, bf16[192,512]{1,0:T(8,128)(2,1)S(1)}, u32[]{:S(2)}, u32[]{:S(2)}) collective-permute-start(bf16[192,512]{1,0:T(8,128)(2,1)S(1)} %hidden.3), channel_id=1, source_target_pairs={{0,1},{1,0},{2,3},{3,2},{4,5},{5,4},{6,7},{7,6},{8,9},{9,8},{10,11... | collective-permute-start | bytes 589832 | tf_op jit(solution)/shard_map/ppermute | solution.py:196

commit v7 on v6

--- a/solution.py
+++ b/solution.py
@@ -35,11 +35,11 @@
     visible = (positions[None, :] < cache_lengths[:, None])[:, None, :]
     highest = jnp.max(jnp.where(visible, scores, -jnp.inf), axis=2, keepdims=True)
     powers = jnp.where(visible, jnp.exp(scores - highest), 0.0)
-    attention_weights = (powers / jnp.sum(powers, axis=2, keepdims=True)).astype(BF16)
     latents = latent_cache[:, :, :LAT]
-    return jnp.einsum(
-        "rhj,rjl->rhl", attention_weights, latents, preferred_element_type=F32
-    ).astype(BF16)
+    summed = jnp.einsum(
+        "rhj,rjl->rhl", powers.astype(BF16), latents, preferred_element_type=F32
+    )
+    return (summed / jnp.sum(powers, axis=2, keepdims=True)).astype(BF16)
 
 
 def dot(a, b, contract=((1,), (0,))):
@@ -100,9 +100,7 @@
     wanted_t_ref[...] = wanted_places(wanted_t_ref.shape, 1)
 
 
-def select_kernel(
-    input_ref, ids_ref, gates_ref, lanes_ref, wanted_ref, wanted_t_ref, send_ref, mix_ref
-):
+def pick_kernel(ids_ref, gates_ref, lanes_ref, wanted_ref, wanted_t_ref, pick_ref, mix_ref):
     ids, gates = ids_ref[...].astype(F32), gates_ref[...].astype(F32)
     lane = index_of((ROWS, EXPERTS), 1)
     member = jnp.zeros(lane.shape, F32)
@@ -116,21 +114,23 @@
     place = jnp.where(member > 0.0, rank, -1.0)
     place = jnp.concatenate([place] * FOLD, axis=0).astype(BF16)
     gate = jnp.concatenate([gate] * FOLD, axis=0).astype(BF16)
-    folded = jnp.concatenate(
-        [input_ref[:, k * WIDTH : (k + 1) * WIDTH] for k in range(FOLD)], axis=0
-    )
-    half = CELLS * MESSAGE
     lanes = lanes_ref[...]
     chosen = dot(lanes, place, ((1,), (1,))) == wanted_ref[...]
-    pick = jnp.where(chosen, 1.0, 0.0).astype(BF16)
-    for h in range(2):
-        picked = dot(pick[h * half : (h + 1) * half], folded).astype(BF16)
-        send_ref[h, 0] = picked
-        send_ref[h, 1] = picked
-
+    pick_ref[...] = jnp.where(chosen, 1.0, 0.0).astype(BF16)
     chosen = dot(place, lanes, ((1,), (1,))) == wanted_t_ref[...]
     weight = dot(gate, lanes, ((1,), (1,)))
     mix_ref[...] = jnp.where(chosen, weight, 0.0).astype(BF16)
+
+
+def select_kernel(input_ref, pick_ref, send_ref):
+    folded = jnp.concatenate(
+        [input_ref[:, k * WIDTH : (k + 1) * WIDTH] for k in range(FOLD)], axis=0
+    )
+    half = CELLS * MESSAGE
+    for h in range(2):
+        picked = dot(pick_ref[h * half : (h + 1) * half], folded).astype(BF16)
+        send_ref[h, 0] = picked
+        send_ref[h, 1] = picked
 
 
 def unfold(got_ref, rows_ref):
@@ -209,9 +209,12 @@
         (array(slots, EXPERTS), array(slots, shared, dtype=F32), array(shared, slots, dtype=F32)),
         cost_estimate=cost(8 * 10**9, 4 * SLOTS * D),
     )
-    send, mix = call(
-        select_kernel, "select", (array(2, 2, CELLS * MESSAGE, WIDTH), array(shared, slots)),
-        expert_input, expert_ids, route_gates, *tables,
+    pick, mix = call(
+        pick_kernel, "pick", (array(slots, shared), array(shared, slots)),
+        expert_ids, route_gates, *tables, cost_estimate=cost(2 * 10**9, 4 * SLOTS * D),
+    )
+    send = call(
+        select_kernel, "select", array(2, 2, CELLS * MESSAGE, WIDTH), expert_input, pick,
         cost_estimate=cost(8 * 10**9, 4 * SLOTS * D),
     )
     got = exchange(send).reshape(SLOTS * FOLD, WIDTH)

time: 107 us -> 107 us (level)
    pallas_call x6 -> x7, Pallas kernels: 14.2 us -> 14.2 us  [call(): pl.pallas_call(kernel, in_specs=[pl.BlockSpec(memory_space=pltpu.SMEM)] *...]
  transfers between devices with their start and end apart: 3 -> 3, of which waited for: 0 -> 1; matrix products, arithmetic and copies ran while one was open for 3% -> 2% of each run, Pallas kernels for 8% -> 8%
where the time goes in v7:
time: 107 us; the launch traced here: 106 us
  blocking collectives  87.7 us (82%)
  Pallas kernels  14.2 us (13%)
  matrix products  2.19 us (2%)
    all_to_all x2, blocking collectives, exchange(): lax.all_to_all(values, ALL, split_axis=0, concat_axis=0, axis_index_group...  87.7 us
    pallas_call x7, Pallas kernels, call(): pl.pallas_call(kernel, in_specs=[pl.BlockSpec(memory_space=pltpu.SMEM)] *...  14.2 us
  transfers between devices with their start and end apart: 3, of which 1 were waited for; matrix products, arithmetic and copies ran while one was open for 2% of the time, Pallas kernels for 8%

profile of v7, /device:TPU:0, one launch (start us, length us, event | category | flops | bytes accessed | tf_op | source)
XLA Modules:
  0.0 106.5 jit_solution(10070723132536965946)
XLA Ops:
  0.6 0.0 copy-start
  0.6 0.0 copy-start.3
  0.7 0.0 copy-start.2
  0.7 0.1 collective-permute-start.2
  0.8 0.0 copy-start.1
  0.8 0.4 tables.1
  1.2 0.2 copy-done.3
  1.4 0.0 copy-done.2
  1.4 0.5 pick.1
  1.9 0.0 copy-done.1
  1.9 0.0 slice-start.1
  1.9 0.0 slice-start.3
  1.9 0.5 select.1
  2.4 0.0 copy-start.5
  2.4 0.0 copy-start.4
  2.5 45.5 %all_to_all.10 = bf16[64,24,896]{2,1,0:T(8,128)(2,1)S(1)} all-to-all(bf16[64,24,896]{2,1,0:T(8,128)(2,1)S(1)} %bitcast.17), channel_id=1, replica_groups={{126,118,110,102,94,86,78,70,62,54,46,38,30,22,14,6,124,116,108,100,92,..., dimensions={0} | all-to-all | bytes 5505024 | tf_op jit(solution)/shard_map/all_to_all | solution.py:190
  48.0 0.0 collective-permute-start
  48.0 0.1 iota_compare_fusion
  48.0 0.6 convolution_multiply_fusion
  48.7 0.4 fusion.21
  49.1 0.0 slice-start.4
  49.1 3.8 %hidden.2.own_ref = bf16[192,512]{1,0:T(8,128)(2,1)S(1)} custom-call(bf16[1536,896]{1,0:T(8,128)(2,1)S(1)} %bitcast.13, bf16[7168,512]{1,0:T(8,128)(2,1)S(1)} %bitcast.8, bf16[7168,512]{1,0:T(8,128)(2,1)S(1)} %bitcast.10), custom_call_target="tpu_custom_call" | custom-call | flops 2818572288 | bytes 14680064 | tf_op jit(solution)/shard_map/hidden/pallas_call | solution.py:63
  53.0 0.0 slice-start.5
  53.0 0.1 collective-permute-done.got_ref
  53.1 3.8 %hidden.3 = bf16[192,512]{1,0:T(8,128)(2,1)S(1)} custom-call(bf16[1536,896]{1,0:T(8,128)(2,1)S(1)} %collective-permute-done.got_ref, bf16[7168,512]{1,0:T(8,128)(2,1)S(1)} %bitcast.8, bf16[7168,512]{1,0:T(8,128)(2,1)S(1)} %bitcast.10), custom_call_target="tpu_custom_call" | custom-call | flops 2818572288 | bytes 14680064 | tf_op jit(solution)/shard_map/hidden/pallas_call | solution.py:63
  56.9 0.7 collective-permute-start.1
  57.6 1.5 %fusion.14 = bf16[2,128,512]{2,1,0:T(8,128)(2,1)} fusion(bf16[2,1024,576]{1,2,0:T(8,128)(2,1)S(1)} %copy-done.4, bf16[2,128,1024]{2,1,0:T(8,128)(2,1)S(1)} %get-tuple-element.25, f32[2,128]{1,0:T(2,128)S(1)} %get-tuple-element.24), kind=kOutput, calls=%fused_computation.10 | convolution fusion | flops 268697600 | bytes 2884608 | tf_op jit(solution)/shard_map/rhj,rjl->rhl/dot_general | solution.py:39
  59.1 0.0 collective-permute-done.1.other_ref
  59.1 0.0 collective-permute-done.2.other_down
  59.1 3.9 %down.1 = bf16[1536,896]{1,0:T(8,128)(2,1)S(1)} custom-call(bf16[192,512]{1,0:T(8,128)(2,1)S(1)} %hidden.2.own_ref, bf16[192,512]{1,0:T(8,128)(2,1)S(1)} %collective-permute-done.1.other_ref, bf16[512,7168]{1,0:T(8,128)(2,1)S(1)} %bitcast.16, bf16[512,7168]{1,0:T(8,128)(2,1)S(1)} %collective-permute-done.2.other_down), custom_call_target="tpu_custom_call" | custom-call | flops 2818572288 | bytes 14680064 | tf_op jit(solution)/shard_map/down/pallas_call | solution.py:63
  63.1 42.2 %all_to_all.11 = bf16[64,24,896]{2,1,0:T(8,128)(2,1)S(1)} all-to-all(bf16[64,24,896]{2,1,0:T(8,128)(2,1)S(1)} %bitcast.14), channel_id=1, replica_groups={{126,118,110,102,94,86,78,70,62,54,46,38,30,22,14,6,124,116,108,100,92,..., dimensions={0} | all-to-all | bytes 5505024 | tf_op jit(solution)/shard_map/all_to_all | solution.py:190
  105.3 1.2 %combine.1 = bf16[8,7168]{1,0:T(8,128)(2,1)} custom-call(bf16[64,768]{1,0:T(8,128)(2,1)S(1)} %get-tuple-element.21.mix_ref, bf16[4,384,896]{2,1,0:T(8,128)(2,1)S(1)} %bitcast.11), custom_call_target="tpu_custom_call" | custom-call | tf_op jit(solution)/shard_map/combine/pallas_call | solution.py:63
  (14 shorter events, 0.0 us)
Async XLA Ops:
  0.6 47.4 %copy-start = (bf16[2,128,576]{1,2,0:T(8,128)(2,1)S(1)}, bf16[2,128,576]{1,2,0:T(8,128)(2,1)}, u32[]{:S(2)}) copy-start(bf16[2,128,576]{1,2,0:T(8,128)(2,1)} %param.9) | copy-start | bytes 884740
  0.6 0.7 copy-start.3
  0.7 0.7 copy-start.2
  0.7 58.5 %collective-permute-start.2 = (bf16[512,7168]{1,0:T(8,128)(2,1)}, bf16[512,7168]{1,0:T(8,128)(2,1)S(1)}, u32[]{:S(2)}, u32[]{:S(2)}) collective-permute-start(bf16[512,7168]{1,0:T(8,128)(2,1)} %own_down.1), channel_id=1, source_target_pairs={{0,1},{1,0},{2,3},{3,2},{4,5},{5,4},{6,7},{7,6},{8,9},{9,8},{10,11... | collective-permute-start | bytes 22020104 | tf_op jit(solution)/shard_map/ppermute | solution.py:196
  0.8 1.1 %copy-start.1 = (bf16[8,7168]{1,0:T(8,128)(2,1)S(1)}, bf16[8,7168]{1,0:T(8,128)(2,1)}, u32[]{:S(2)}) copy-start(bf16[8,7168]{1,0:T(8,128)(2,1)} %input_ref.1) | copy-start | bytes 344068
  1.4 47.7 %slice-start = ((s8[7340032]{0:T(1024)(128)(4,1)}), s8[4194304]{0:T(1024)(128)(4,1)S(1)}, s32[]{:S(2)}) async-start(s8[7340032]{0:T(1024)(128)(4,1)} %bitcast.7), calls=%async_computation.2 | async-start | bytes 8388608
  1.4 47.7 %slice-start.2 = ((s8[7340032]{0:T(1024)(128)(4,1)}), s8[4194304]{0:T(1024)(128)(4,1)S(1)}, s32[]{:S(2)}) async-start(s8[7340032]{0:T(1024)(128)(4,1)} %bitcast.9), calls=%async_computation.4 | async-start | bytes 8388608
  1.9 47.2 %slice-start.1 = ((s8[7340032]{0:T(1024)(128)(4,1)}), s8[3145728]{0:T(1024)(128)(4,1)S(1)}, s32[]{:S(2)}) async-start(s8[7340032]{0:T(1024)(128)(4,1)} %bitcast.7), calls=%async_computation.3 | async-start | bytes 6291456
  1.9 47.2 %slice-start.3 = ((s8[7340032]{0:T(1024)(128)(4,1)}), s8[3145728]{0:T(1024)(128)(4,1)S(1)}, s32[]{:S(2)}) async-start(s8[7340032]{0:T(1024)(128)(4,1)} %bitcast.9), calls=%async_computation.5 | async-start | bytes 6291456
  2.4 45.5 %copy-start.5 = (s32[2]{0:T(128)S(1)}, s32[2]{0:T(128)}, u32[]{:S(2)}) copy-start(s32[2]{0:T(128)} %param.11) | copy-start | bytes 28
  2.4 45.6 %copy-start.4 = (bf16[2,1024,576]{1,2,0:T(8,128)(2,1)S(1)}, bf16[2,1024,576]{1,2,0:T(8,128)(2,1)}, u32[]{:S(2)}) copy-start(bf16[2,1024,576]{1,2,0:T(8,128)(2,1)} %param.10) | copy-start | bytes 7077892
  48.0 5.1 %collective-permute-start = (bf16[1536,896]{1,0:T(8,128)(2,1)S(1)}, bf16[1536,896]{1,0:T(8,128)(2,1)S(1)}, u32[]{:S(2)}, u32[]{:S(2)}) collective-permute-start(bf16[1536,896]{1,0:T(8,128)(2,1)S(1)} %bitcast.12), channel_id=1, source_target_pairs={{0,1},{1,0},{2,3},{3,2},{4,5},{5,4},{6,7},{7,6},{8,9},{9,8},{10,11... | collective-permute-start | bytes 8257544 | tf_op jit(solution)/shard_map/ppermute | solution.py:196
  49.1 10.0 %slice-start.4 = ((s8[7340032]{0:T(1024)(128)(4,1)}), s8[4194304]{0:T(1024)(128)(4,1)S(1)}, s32[]{:S(2)}) async-start(s8[7340032]{0:T(1024)(128)(4,1)} %bitcast.15), calls=%async_computation.6 | async-start | bytes 8388608
  53.0 6.2 %slice-start.5 = ((s8[7340032]{0:T(1024)(128)(4,1)}), s8[3145728]{0:T(1024)(128)(4,1)S(1)}, s32[]{:S(2)}) async-start(s8[7340032]{0:T(1024)(128)(4,1)} %bitcast.15), calls=%async_computation.7 | async-start | bytes 6291456
  56.9 2.2 %collective-permute-start.1 = (bf16[192,512]{1,0:T(8,128)(2,1)S(1)}, bf16[192,512]{1,0:T(8,128)(2,1)S(1)}, u32[]{:S(2)}, u32[]{:S(2)}) collective-permute-start(bf16[192,512]{1,0:T(8,128)(2,1)S(1)} %hidden.3), channel_id=1, source_target_pairs={{0,1},{1,0},{2,3},{3,2},{4,5},{5,4},{6,7},{7,6},{8,9},{9,8},{10,11... | collective-permute-start | bytes 589832 | tf_op jit(solution)/shard_map/ppermute | solution.py:196
